TPU v7x, 32 devices: a whole 2x2x4 slice. The times are simulated.
32 devices in a mesh: dp: 4 (over y, x), tile: 8 (over z, core).
Axes of the slice: x: 2, y: 2, z: 4, core: 2. Of those that a mesh axis runs over, the one named last changes fastest.
Arguments:
- features: bfloat16 [4, 64, 64, 128], P('dp', None, 'tile'), may hold values from -6 to 6
- occupied_block_mask: int32 [4, 8, 2], P('dp', 'tile'), may hold values 0 or 1
- conv_one: bfloat16 [27, 64, 64], replicated, may hold values from -0.15625 to 0.15625
- conv_two: bfloat16 [27, 64, 64], replicated, may hold values from -0.15625 to 0.15625
- gain: float32 [64], replicated, may hold values from 0.5 to 1.5
- shift: float32 [64], replicated, may hold values from -3 to 3
- cotangent: bfloat16 [4, 64, 64, 128], P('dp', None, 'tile'), may hold values from -6 to 6
Outputs:
- section_out: bfloat16 [4, 64, 64, 128], P('dp', None, 'tile')
- input_grad: bfloat16 [4, 64, 64, 128], P('dp', None, 'tile')
- grad_one: float32 [27, 64, 64], replicated
- grad_two: float32 [27, 64, 64], replicated
- gain_grad: float32 [64], replicated
- shift_grad: float32 [64], replicated
Inputs may be any that keep to these rules, and one draw needn't show every extreme that they name: `occupied_block_mask`: each entry marks whether a block holds points.
All inputs are finite; a program needn't handle non-finite values.
Results may differ from a plain program's by a relative error of at most 0.0034.
Values may be sent and summed in bfloat16 or wider, within the bound.
A program may use at most 128 MiB of HBM per device.

v0:
```python
import functools

import jax
import jax.numpy as jnp
from jax import lax
from jax.experimental import pallas as pl
from jax.experimental.pallas import tpu as pltpu
from jax.sharding import PartitionSpec as P

BLK = 8
LANES = 128
EPSILON = 1e-05
MESH = pl.DeviceIdType.MESH
F32 = jnp.float32
BF16 = jnp.bfloat16


def kernel(
    n_dp, n_tile, ch, nx, hy,
    xd_ref, occ_ref, k1_ref, k2_ref, gain_ref, shift_ref,
    so_ref, ig_ref, q4, sums_out,
    w1_ref, w2_ref, w1f_ref, w2f_ref, xd_pad, a_pad, i_pad, s_x, s_t, d3, ar_a, ar_b, part, rp, half_sum, r1, acc, r2, q3,
    halo_s, halo_r, ar_s, ar_r, rs_s, rs_r,
):
    n_a, n_b = 2 * n_dp, n_tile // 2
    dp, tile = lax.axis_index("dp"), lax.axis_index("tile")
    core, z = lax.rem(tile, 2), tile // 2
    a_me = core * n_dp + dp
    flat = nx * hy
    c_a = part.shape[1] // n_a
    c_b = c_a // n_b

    def peer_a(k):
        other = lax.rem(a_me + k, n_a)
        return other, (lax.rem(other, n_dp), z * 2 + other // n_dp)

    def peer_b(k):
        other = lax.rem(z + k, n_b)
        return other, (dp, other * 2 + core)

    has_left, has_right = tile > 0, tile < n_tile - 1

    barrier = pltpu.get_barrier_semaphore()
    for k in range(1, n_a):
        pl.semaphore_signal(barrier, inc=1, device_id=peer_a(k)[1], device_id_type=MESH)
    for k in range(1, n_b):
        pl.semaphore_signal(barrier, inc=1, device_id=peer_b(k)[1], device_id_type=MESH)

    @pl.when(has_left)
    def _():
        pl.semaphore_signal(barrier, inc=1, device_id=(dp, tile - 1), device_id_type=MESH)

    @pl.when(has_right)
    def _():
        pl.semaphore_signal(barrier, inc=1, device_id=(dp, tile + 1), device_id_type=MESH)

    width = hy // BLK
    spot = lax.broadcasted_iota(jnp.int32, (1, flat), 1)
    block_x, block_y = spot // (hy * BLK), lax.rem(spot, width) // BLK
    mask = jnp.zeros((1, flat), F32)
    for bx in range(nx // BLK):
        for by in range(width // BLK):
            mask = jnp.where((block_x == bx) & (block_y == by),
                             occ_ref[bx, by].astype(F32), mask)
    xd_pad[:, pl.ds(hy, flat)] = (xd_ref[...].astype(F32) * mask).astype(BF16)
    same = (lax.broadcasted_iota(jnp.int32, (ch, ch), 0)
            == lax.broadcasted_iota(jnp.int32, (ch, ch), 1)).astype(BF16)

    def as_matrix(taps, out):
        for a in range(3):
            out[pl.ds(a * ch, ch), :] = lax.dot_general(
                same, taps[pl.ds(a * 9 * ch, 9 * ch), :], (((1,), (1,)), ((), ())),
                preferred_element_type=F32).astype(BF16)

    def as_flipped(taps, out):
        for a in range(3):
            out[pl.ds(a * ch, ch), :] = jnp.concatenate(
                [taps[pl.ds((26 - 9 * a - k) * ch, ch), :] for k in range(9)], axis=1)

    as_matrix(k1_ref, w1_ref)

    sides = has_left.astype(jnp.int32) + has_right.astype(jnp.int32)
    pl.semaphore_wait(barrier, n_a + n_b - 2 + sides)

    def halo(phase, src, first, pad):
        low = pltpu.make_async_remote_copy(
            src_ref=src.at[:, pl.ds(first, hy)],
            dst_ref=pad.at[:, pl.ds(flat + hy, hy)],
            send_sem=halo_s.at[phase, 0], recv_sem=halo_r.at[phase, 0],
            device_id=(dp, tile - 1), device_id_type=MESH)
        high = pltpu.make_async_remote_copy(
            src_ref=src.at[:, pl.ds(first + flat - hy, hy)],
            dst_ref=pad.at[:, pl.ds(0, hy)],
            send_sem=halo_s.at[phase, 1], recv_sem=halo_r.at[phase, 1],
            device_id=(dp, tile + 1), device_id_type=MESH)

        @pl.when(has_left)
        def _():
            low.start()

        @pl.when(has_right)
        def _():
            high.start()

        def finish():
            @pl.when(has_left)
            def _():
                low.wait_send()
                high.wait_recv()

            @pl.when(has_right)
            def _():
                high.wait_send()
                low.wait_recv()

        return finish

    def zero_ends(pad):
        @pl.when(jnp.logical_not(has_left))
        def _():
            pad[:, pl.ds(0, hy)] = jnp.zeros((pad.shape[0], hy), pad.dtype)

        @pl.when(jnp.logical_not(has_right))
        def _():
            pad[:, pl.ds(flat + hy, hy)] = jnp.zeros((pad.shape[0], hy), pad.dtype)

    lane = lax.broadcasted_iota(jnp.int32, (1, hy), 1)
    row_h, row_y = lane // width, lax.rem(lane, width)

    def shifts(pad, first, out, inner=True, outer=True):
        def plane(x, carry):
            at = pl.ds(x * hy if isinstance(x, int) else pl.multiple_of(x * hy, hy), hy)
            values = pad[pl.ds(first, ch), at]
            for b in range(3):
                for c in range(3):
                    step = (b - 1) * width + (c - 1)
                    moved = values
                    if step:
                        moved = pltpu.roll(values, (-step) % hy, 1)
                        fits = ((row_h + (b - 1) >= 0) & (row_h + (b - 1) < BLK)
                                & (row_y + (c - 1) >= 0) & (row_y + (c - 1) < width))
                        moved = jnp.where(fits, moved, jnp.zeros_like(moved))
                    out[pl.ds((3 * b + c) * ch, ch), at] = moved.astype(BF16)
            return carry
        if inner:
            lax.fori_loop(1, nx + 1, plane, 0, unroll=True)
        if outer:
            plane(0, 0)
            plane(nx + 1, 0)

    def conv(weight, stack):
        grown = jnp.dot(weight[...], stack[...], preferred_element_type=F32)
        return (grown[:ch, :flat] + grown[ch:2 * ch, hy:hy + flat]
                + grown[2 * ch:, 2 * hy:2 * hy + flat])

    def kernel_grad(stack, g):
        dims = (((1,), (1,)), ((), ()))
        rows = 9 * ch
        half = rows // 2
        part[g, pl.ds(0, rows), :] = lax.dot_general(
            stack[...], d3[pl.ds(0, 2 * ch), :], dims, preferred_element_type=F32)
        rest = lax.dot_general(
            stack[...], d3[pl.ds(2 * ch, ch), :], dims, preferred_element_type=F32)
        part[g, pl.ds(rows, half), :] = jnp.concatenate([rest[:half], rest[half:]], axis=1)

    def put_d3(value):
        for a in range(3):
            d3[pl.ds(a * ch, ch), pl.ds(a * hy, flat)] = value

    def to_rows(columns):
        spot = lax.broadcasted_iota(jnp.int32, (ch, LANES), 1)
        block = jnp.zeros((ch, LANES), F32)
        for index, column in enumerate(columns):
            block = jnp.where(spot == index, column, block)
        return jnp.transpose(block)[:8]

    def to_columns(rows):
        return jnp.transpose(jnp.concatenate([rows, jnp.zeros((LANES - 8, ch), F32)], axis=0))

    def spread(call, slots, mine, peers, size, base):
        copies = []
        for k in range(1, size):
            copy = pltpu.make_async_remote_copy(
                src_ref=slots.at[call, mine], dst_ref=slots.at[call, mine],
                send_sem=ar_s.at[call, base + k], recv_sem=ar_r.at[call, base + k],
                device_id=peers(k)[1], device_id_type=MESH)
            copy.start()
            copies.append(copy)
        return copies

    def wait_all(copies):
        for copy in copies:
            copy.wait()

    def small_start(call, rows):
        ar_a[call, a_me] = rows
        return spread(call, ar_a, a_me, peer_a, n_a, 0)

    def small_next(call, copies, merge):
        wait_all(copies)
        ar_b[call, z] = merge([ar_a[call, k] for k in range(n_a)])
        return spread(call, ar_b, z, peer_b, n_b, n_a)

    def small_end(call, copies, merge):
        wait_all(copies)
        return merge([ar_b[call, k] for k in range(n_b)])

    def add(rows):
        total = rows[0]
        for row in rows[1:]:
            total = total + row
        return total

    def merge_moments(rows):
        total = add(rows)
        count, sums = total[2:3], total[0:1]
        mean = sums / jnp.maximum(count, 1.0)
        spread_all = total[1:2]
        for row in rows:
            off = row[0:1] / jnp.maximum(row[2:3], 1.0) - mean
            spread_all = spread_all + row[2:3] * off * off
        return jnp.concatenate([sums, spread_all, count, jnp.zeros((5, ch), F32)], axis=0)

    half_rows = part.shape[1] // 2

    def scatter_core(g):
        theirs = pl.ds(pl.multiple_of((1 - core) * half_rows, half_rows), half_rows)
        copy = pltpu.make_async_remote_copy(
            src_ref=part.at[g, theirs, :], dst_ref=rp.at[g],
            send_sem=rs_s.at[g, 0], recv_sem=rs_r.at[g, 0],
            device_id=(dp, z * 2 + 1 - core), device_id_type=MESH)
        copy.start()
        return [copy]

    def scatter_a(g, copies):
        wait_all(copies)
        mine = pl.ds(pl.multiple_of(core * half_rows, half_rows), half_rows)
        half_sum[g] = part[g, mine, :] + rp[g]
        copies = []
        for k in range(1, n_dp):
            other = lax.rem(dp + k, n_dp)
            copy = pltpu.make_async_remote_copy(
                src_ref=half_sum.at[g, pl.ds(pl.multiple_of(other * c_a, c_a), c_a), :],
                dst_ref=r1.at[g, k - 1],
                send_sem=rs_s.at[g, k], recv_sem=rs_r.at[g, k],
                device_id=(other, tile), device_id_type=MESH)
            copy.start()
            copies.append(copy)
        return copies

    def scatter_b(g, copies):
        wait_all(copies)
        total = half_sum[g, pl.ds(pl.multiple_of(dp * c_a, c_a), c_a), :]
        for k in range(1, n_dp):
            total = total + r1[g, k - 1]
        acc[g] = total
        copies = []
        for k in range(1, n_b):
            other, device = peer_b(k)
            copy = pltpu.make_async_remote_copy(
                src_ref=acc.at[g, pl.ds(pl.multiple_of(other * c_b, c_b), c_b), :],
                dst_ref=r2.at[g, k - 1],
                send_sem=rs_s.at[g, n_a + k], recv_sem=rs_r.at[g, n_a + k],
                device_id=device, device_id_type=MESH)
            copy.start()
            copies.append(copy)
        return copies

    def gather_b(g, copies):
        wait_all(copies)
        mine = pl.ds(pl.multiple_of(z * c_b, c_b), c_b)
        total = acc[g, mine, :]
        for k in range(1, n_b):
            total = total + r2[g, k - 1]
        q3[g, mine, :] = total.astype(BF16)
        copies = []
        for k in range(1, n_b):
            copy = pltpu.make_async_remote_copy(
                src_ref=q3.at[g, mine, :], dst_ref=q3.at[g, mine, :],
                send_sem=rs_s.at[g, n_a + n_b + k], recv_sem=rs_r.at[g, n_a + n_b + k],
                device_id=peer_b(k)[1], device_id_type=MESH)
            copy.start()
            copies.append(copy)
        return copies

    def gather_a(g, copies):
        wait_all(copies)
        mine = pl.ds(pl.multiple_of(a_me * c_a, c_a), c_a)
        copies = []
        for k in range(1, n_a):
            copy = pltpu.make_async_remote_copy(
                src_ref=q3.at[g], dst_ref=q4.at[g, mine, :],
                send_sem=rs_s.at[g, n_a + 2 * n_b + k], recv_sem=rs_r.at[g, n_a + 2 * n_b + k],
                device_id=peer_a(k)[1], device_id_type=MESH)
            copy.start()
            copies.append(copy)
        q4[g, mine, :] = q3[g]
        return copies

    end_xd = halo(0, xd_pad, hy, xd_pad)
    shifts(xd_pad, 0, s_x, outer=False)
    zero_ends(xd_pad)
    zero_ends(a_pad)
    zero_ends(i_pad)
    end_xd()

    shifts(xd_pad, 0, s_x, inner=False)
    pre = conv(w1_ref, s_x)
    count_here = jnp.sum(mask, axis=1, keepdims=True)
    sums_here = jnp.sum(pre * mask, axis=1, keepdims=True)
    off = (pre - sums_here / jnp.maximum(count_here, 1.0)) * mask
    squares_here = jnp.sum(off * off, axis=1, keepdims=True)
    copies = small_start(0, to_rows([sums_here, squares_here, count_here]))

    shifts(xd_pad, ch, s_t)
    as_flipped(k2_ref, w2f_ref)
    act_grad = conv(w2f_ref, s_t)
    gain_shift = to_columns(jnp.concatenate(
        [gain_ref[...], shift_ref[...], jnp.zeros((6, ch), F32)], axis=0))

    copies = small_next(0, copies, merge_moments)
    d3[...] = jnp.zeros(d3.shape, d3.dtype)
    put_d3(xd_pad[pl.ds(ch, ch), pl.ds(hy, flat)])
    used = 27 * ch // 2
    for g in range(2):
        part[g, pl.ds(used, part.shape[1] - used), :] = jnp.zeros(
            (part.shape[1] - used, LANES), F32)
    moments = to_columns(small_end(0, copies, merge_moments))
    count = moments[:, 2:3]
    mean = moments[:, 0:1] / count
    inv_std = lax.rsqrt(moments[:, 1:2] / count + EPSILON)
    gain, shift = gain_shift[:, 0:1], gain_shift[:, 1:2]
    normal = (pre - mean) * inv_std
    pre_act = gain * normal + shift
    sg = 1.0 / (1.0 + jnp.exp(-pre_act))
    a_pad[:, pl.ds(hy, flat)] = (pre_act * sg * mask).astype(BF16)
    end_act = halo(1, a_pad, hy, a_pad)
    z_grad = act_grad * mask * sg * (1.0 + pre_act * (1.0 - sg))
    shift_here = jnp.sum(z_grad, axis=1, keepdims=True)
    gain_here = jnp.sum(z_grad * normal, axis=1, keepdims=True)
    copies = small_start(1, to_rows([shift_here, gain_here]))

    as_matrix(k2_ref, w2_ref)
    as_flipped(k1_ref, w1f_ref)
    shifts(a_pad, 0, s_t, outer=False)
    end_act()
    shifts(a_pad, 0, s_t, inner=False)
    copies = small_next(1, copies, add)
    kernel_grad(s_t, 0)
    two = scatter_core(0)
    totals = small_end(1, copies, add)
    sums_out[...] = totals
    totals = to_columns(totals)
    delta_one = (gain * inv_std * (
        z_grad - totals[:, 0:1] / count - normal * (totals[:, 1:2] / count)) * mask).astype(BF16)
    i_pad[:, pl.ds(hy, flat)] = delta_one
    end_delta = halo(2, i_pad, hy, i_pad)
    put_d3(delta_one)
    kernel_grad(s_x, 1)
    one = scatter_core(1)
    two = scatter_a(0, two)
    pre_two = conv(w2_ref, s_t)
    so_ref[...] = ((xd_pad[pl.ds(0, ch), pl.ds(hy, flat)].astype(F32) + pre_two) * mask).astype(BF16)
    one = scatter_a(1, one)
    two = scatter_b(0, two)
    shifts(i_pad, 0, s_t, outer=False)
    end_delta()
    shifts(i_pad, 0, s_t, inner=False)
    one = scatter_b(1, one)
    two = gather_b(0, two)
    back = conv(w1f_ref, s_t)
    ig_ref[...] = ((xd_pad[pl.ds(ch, ch), pl.ds(hy, flat)].astype(F32) + back) * mask).astype(BF16)
    one = gather_b(1, one)
    two = gather_a(0, two)
    one = gather_a(1, one)
    wait_all(one)
    wait_all(two)


def unpack(ch, so_in, ig_in, q4, sums, so_ref, ig_ref, g1_ref, g2_ref, gain_ref, shift_ref):
    rows = 9 * ch
    half = rows // 2
    for g, out in ((1, g1_ref), (0, g2_ref)):
        for a in range(2):
            out[pl.ds(a * rows, rows), :] = q4[g, pl.ds(0, rows), pl.ds(a * ch, ch)].astype(F32)
        for side in range(2):
            out[pl.ds(2 * rows + side * half, half), :] = (
                q4[g, pl.ds(rows, half), pl.ds(side * ch, ch)].astype(F32))
    so_ref[...] = so_in[...]
    ig_ref[...] = ig_in[...]
    shift_ref[...] = sums[0:1, :]
    gain_ref[...] = sums[1:2, :]


def local(n_dp, n_tile, features, occupied, conv_one, conv_two, gain, shift, cotangent):
    scenes, ch, nx, hy = features.shape
    flat = nx * hy
    xd = jnp.concatenate([features.reshape(ch, flat), cotangent.reshape(ch, flat)], axis=0)
    n_a, n_b = 2 * n_dp, n_tile // 2
    c_b = -(-(27 * ch // 2) // (n_a * n_b * 16)) * 16
    c_a = c_b * n_b
    rows = c_a * n_a
    vmem = pl.BlockSpec(memory_space=pltpu.VMEM)
    dma = pltpu.SemaphoreType.DMA
    so, ig, q4, sums = pl.pallas_call(
        functools.partial(kernel, n_dp, n_tile, ch, nx, hy),
        out_shape=(
            jax.ShapeDtypeStruct((ch, flat), BF16),
            jax.ShapeDtypeStruct((ch, flat), BF16),
            jax.ShapeDtypeStruct((2, rows, LANES), BF16),
            jax.ShapeDtypeStruct((8, ch), F32),
        ),
        in_specs=[vmem, pl.BlockSpec(memory_space=pltpu.SMEM)] + [vmem] * 4,
        out_specs=[vmem] * 4,
        scratch_shapes=[
            pltpu.VMEM((3 * ch, 9 * ch), BF16),
            pltpu.VMEM((3 * ch, 9 * ch), BF16),
            pltpu.VMEM((3 * ch, 9 * ch), BF16),
            pltpu.VMEM((3 * ch, 9 * ch), BF16),
            pltpu.VMEM((2 * ch, flat + 2 * hy), BF16),
            pltpu.VMEM((ch, flat + 2 * hy), BF16),
            pltpu.VMEM((ch, flat + 2 * hy), BF16),
            pltpu.VMEM((9 * ch, flat + 2 * hy), BF16),
            pltpu.VMEM((9 * ch, flat + 2 * hy), BF16),
            pltpu.VMEM((3 * ch, flat + 2 * hy), BF16),
            pltpu.VMEM((2, n_a, 8, ch), F32),
            pltpu.VMEM((2, n_b, 8, ch), F32),
            pltpu.VMEM((2, rows, LANES), F32),
            pltpu.VMEM((2, rows // 2, LANES), F32),
            pltpu.VMEM((2, rows // 2, LANES), F32),
            pltpu.VMEM((2, n_dp - 1, c_a, LANES), F32),
            pltpu.VMEM((2, c_a, LANES), F32),
            pltpu.VMEM((2, n_b - 1, c_b, LANES), F32),
            pltpu.VMEM((2, c_a, LANES), BF16),
            dma((3, 2)), dma((3, 2)),
            dma((2, n_a + n_b)), dma((2, n_a + n_b)),
            dma((2, 2 * (n_a + n_b))), dma((2, 2 * (n_a + n_b))),
        ],
        compiler_params=pltpu.CompilerParams(
            collective_id=0, has_side_effects=True, vmem_limit_bytes=48 * 2**20),
    )(
        xd, occupied[0], conv_one.reshape(27 * ch, ch), conv_two.reshape(27 * ch, ch),
        gain.reshape(1, ch), shift.reshape(1, ch),
    )
    planes = features.shape[1:]
    so, ig, g1, g2, gg, sg = pl.pallas_call(
        functools.partial(unpack, ch),
        out_shape=(
            jax.ShapeDtypeStruct(planes, BF16),
            jax.ShapeDtypeStruct(planes, BF16),
            jax.ShapeDtypeStruct((27 * ch, ch), F32),
            jax.ShapeDtypeStruct((27 * ch, ch), F32),
            jax.ShapeDtypeStruct((1, ch), F32),
            jax.ShapeDtypeStruct((1, ch), F32),
        ),
        in_specs=[vmem] * 4,
        out_specs=[vmem] * 6,
        compiler_params=pltpu.CompilerParams(vmem_limit_bytes=16 * 2**20),
    )(so.reshape(planes), ig.reshape(planes), q4, sums)
    shape = features.shape
    return (so.reshape(shape), ig.reshape(shape), g1.reshape(27, ch, ch),
            g2.reshape(27, ch, ch), gg.reshape(ch), sg.reshape(ch))


def solution(mesh):
    split = P("dp", None, "tile", None)
    return jax.shard_map(
        functools.partial(local, mesh.shape["dp"], mesh.shape["tile"]),
        mesh=mesh,
        in_specs=(split, P("dp", "tile", None), P(), P(), P(), P(), split),
        out_specs=(split, split, P(), P(), P(), P()),
        check_vma=False,
    )
```

profile of v0, /device:TPU:0, one launch (start us, length us, event | category | flops | bytes accessed | tf_op | source)
XLA Modules:
  0.0 48.0 jit_solution(12467413298868787347)
XLA Ops:
  0.6 0.0 copy-start
  0.6 0.0 copy-start.1
  0.7 1.1 %copy_bitcast_fusion = (bf16[64,1024]{1,0:T(8,128)(2,1)S(1)}, bf16[64,1024]{1,0:T(8,128)(2,1)S(1)}) fusion(bf16[8,8,8,128]{3,2,1,0:T(8,128)(2,1)} %bitcast.32, bf16[8,8,8,128]{3,2,1,0:T(8,128)(2,1)} %bitcast.33), kind=kLoop, calls=%fused_computation.1 | loop fusion | bytes 524288 | tf_op jit(solution)/shard_map/reshape | solution.py:398
  1.7 0.0 copy-start.2
  1.7 0.0 copy-start.3
  1.8 0.0 copy-start.4
  1.8 0.0 copy-done
  1.8 0.1 copy-done.1
  1.9 0.5 %copy-done.2 = s32[1,1,2]{2,1,0:T(1,128)S(1)} copy-done((s32[1,1,2]{2,1,0:T(1,128)S(1)}, s32[1,1,2]{2,1,0:T(1,128)}, u32[]{:S(2)}) %copy-start.2) | copy-done | bytes 32
  2.4 0.0 copy-done.3
  2.4 0.0 copy-done.4
  2.5 44.1 %shard_map.118 = (bf16[64,1024]{1,0:T(8,128)(2,1)S(1)}, bf16[64,1024]{1,0:T(8,128)(2,1)S(1)}, bf16[2,1024,128]{2,1,0:T(8,128)(2,1)S(1)}, f32[8,64]{1,0:T(8,128)S(1)}) custom-call(bf16[128,1024]{1,0:T(8,128)(2,1)S(1)} %pad_maximum_fusion.xd_ref, s32[1,2]{1,0:T(1,128)S(1)} %bitcast.29, bf16[1728,64]{1,0:T(8,128)(2,1)S(1)} %bitcast.25, ...), custom_call_target="tpu_custom_call" | custom-call | tf_op jit(solution)/shard_map/pallas_call | solution.py:405
  46.6 1.4 %shard_map.119 = (bf16[64,8,128]{2,1,0:T(8,128)(2,1)}, bf16[64,8,128]{2,1,0:T(8,128)(2,1)}, f32[1728,64]{1,0:T(8,128)}, f32[1728,64]{1,0:T(8,128)}, f32[1,64]{1,0:T(1,128)}, /*index=5*/f32[1,64]{1,0:T(1,128)}) custom-call(bf16[64,8,128]{2,1,0:T(8,128)(2,1)S(1)} %bitcast.23, bf16[64,8,128]{2,1,0:T(8,128)(2,1)S(1)} %bitcast.24, ...), custom_call_target="tpu_custom_call" | custom-call | tf_op jit(solution)/shard_map/pallas_call | solution.py:446
  (3 shorter events, 0.1 us)
Async XLA Ops:
  0.6 1.2 %copy-start = (bf16[27,64,64]{2,1,0:T(8,128)(2,1)S(1)}, bf16[27,64,64]{2,1,0:T(8,128)(2,1)}, u32[]{:S(2)}) copy-start(bf16[27,64,64]{2,1,0:T(8,128)(2,1)} %param.9) | copy-start | bytes 663556
  0.6 1.3 %copy-start.1 = (bf16[27,64,64]{2,1,0:T(8,128)(2,1)S(1)}, bf16[27,64,64]{2,1,0:T(8,128)(2,1)}, u32[]{:S(2)}) copy-start(bf16[27,64,64]{2,1,0:T(8,128)(2,1)} %param.10) | copy-start | bytes 663556
  1.7 0.7 %copy-start.2 = (s32[1,1,2]{2,1,0:T(1,128)S(1)}, s32[1,1,2]{2,1,0:T(1,128)}, u32[]{:S(2)}) copy-start(s32[1,1,2]{2,1,0:T(1,128)} %param.8) | copy-start | bytes 28
  1.7 0.7 %copy-start.3 = (f32[64]{0:T(128)S(1)}, f32[64]{0:T(128)}, u32[]{:S(2)}) copy-start(f32[64]{0:T(128)} %param.11) | copy-start | bytes 772
  1.8 0.7 %copy-start.4 = (f32[64]{0:T(128)S(1)}, f32[64]{0:T(128)}, u32[]{:S(2)}) copy-start(f32[64]{0:T(128)} %param.12) | copy-start | bytes 772
where the time goes:
time: 48.2 us; the launch traced here: 48 us
  Pallas kernels  45.5 us (94%)
  local copies, waits for them, and re-layouts  1.78 us (4%)
  between operations  0.72 us (1%)
    pallas_call x1, Pallas kernels, local(): pl.pallas_call(functools.partial(kernel, n_dp, n_tile, ch, nx, hy), out_s...  44.1 us
    pallas_call x1, Pallas kernels, local(): pl.pallas_call(functools.partial(unpack, ch), out_shape=(jax.ShapeDtypeSt...  1.42 us
    reshape x1, local copies, waits for them, and re-layouts, local(): cotangent.reshape(ch, flat)  1.07 us

commit v1 on v0

v1 whole, which is shorter than its diff:
```python
import functools

import jax
import jax.numpy as jnp
from jax import lax
from jax.experimental import pallas as pl
from jax.experimental.pallas import tpu as pltpu
from jax.sharding import PartitionSpec as P

BLK = 8
LANES = 128
EPSILON = 1e-05
MESH = pl.DeviceIdType.MESH
F32 = jnp.float32
BF16 = jnp.bfloat16


def kernel(
    n_dp, n_tile, ch, nx, hy,
    xd_ref, occ_ref, k1_ref, k2_ref, gain_ref, shift_ref,
    so_ref, ig_ref, q4, sums_out,
    w1_ref, w2_ref, w1f_ref, w2f_ref, xd_pad, a_pad, i_pad, s_x, s_d, s_t, d3, ar, part, rp, half, r1,
    halo_s, halo_r, ar_s, ar_r, rs_s, rs_r,
):
    n_z = n_tile // 2
    n_chips, n_all = n_dp * n_z, n_dp * n_tile
    dp, tile = lax.axis_index("dp"), lax.axis_index("tile")
    core, z = lax.rem(tile, 2), tile // 2
    me, chip = dp * n_tile + tile, dp * n_z + z
    flat = nx * hy
    rows_half = half.shape[1]
    size = r1.shape[2]
    owners = rows_half // size

    def each(count, body):
        def step(k, carry):
            body(k)
            return carry
        lax.fori_loop(1, count, step, 0, unroll=count <= 32)

    def peer(k):
        other = lax.rem(me + k, n_all)
        return (other // n_tile, lax.rem(other, n_tile))

    def chip_peer(k):
        other = lax.rem(chip + k, n_chips)
        return other, (other // n_z, lax.rem(other, n_z) * 2 + core)

    sibling = (dp, z * 2 + 1 - core)
    has_left, has_right = tile > 0, tile < n_tile - 1

    barrier = pltpu.get_barrier_semaphore()
    each(n_all, lambda k: pl.semaphore_signal(
        barrier, inc=1, device_id=peer(k), device_id_type=MESH))

    width = hy // BLK
    spot = lax.broadcasted_iota(jnp.int32, (1, flat), 1)
    block_x, block_y = spot // (hy * BLK), lax.rem(spot, width) // BLK
    mask = jnp.zeros((1, flat), F32)
    for bx in range(nx // BLK):
        for by in range(width // BLK):
            mask = jnp.where((block_x == bx) & (block_y == by),
                             occ_ref[bx, by].astype(F32), mask)
    xd_pad[:, pl.ds(hy, flat)] = (xd_ref[...].astype(F32) * mask).astype(BF16)
    same = (lax.broadcasted_iota(jnp.int32, (ch, ch), 0)
            == lax.broadcasted_iota(jnp.int32, (ch, ch), 1)).astype(BF16)

    def as_matrix(taps, out):
        for a in range(3):
            out[pl.ds(a * ch, ch), :] = lax.dot_general(
                same, taps[pl.ds(a * 9 * ch, 9 * ch), :], (((1,), (1,)), ((), ())),
                preferred_element_type=F32).astype(BF16)

    def as_flipped(taps, out):
        for a in range(3):
            out[pl.ds(a * ch, ch), :] = jnp.concatenate(
                [taps[pl.ds((26 - 9 * a - k) * ch, ch), :] for k in range(9)], axis=1)

    as_matrix(k1_ref, w1_ref)

    pl.semaphore_wait(barrier, n_all - 1)

    def halo(phase, src, first, pad):
        low = pltpu.make_async_remote_copy(
            src_ref=src.at[:, pl.ds(first, hy)],
            dst_ref=pad.at[:, pl.ds(flat + hy, hy)],
            send_sem=halo_s.at[phase, 0], recv_sem=halo_r.at[phase, 0],
            device_id=(dp, tile - 1), device_id_type=MESH)
        high = pltpu.make_async_remote_copy(
            src_ref=src.at[:, pl.ds(first + flat - hy, hy)],
            dst_ref=pad.at[:, pl.ds(0, hy)],
            send_sem=halo_s.at[phase, 1], recv_sem=halo_r.at[phase, 1],
            device_id=(dp, tile + 1), device_id_type=MESH)

        @pl.when(has_left)
        def _():
            low.start()

        @pl.when(has_right)
        def _():
            high.start()

        def finish():
            @pl.when(has_left)
            def _():
                low.wait_send()
                high.wait_recv()

            @pl.when(has_right)
            def _():
                high.wait_send()
                low.wait_recv()

        return finish

    def zero_ends(pad):
        @pl.when(jnp.logical_not(has_left))
        def _():
            pad[:, pl.ds(0, hy)] = jnp.zeros((pad.shape[0], hy), pad.dtype)

        @pl.when(jnp.logical_not(has_right))
        def _():
            pad[:, pl.ds(flat + hy, hy)] = jnp.zeros((pad.shape[0], hy), pad.dtype)

    lane = lax.broadcasted_iota(jnp.int32, (1, hy), 1)
    row_h, row_y = lane // width, lax.rem(lane, width)

    def shifts(pad, first, out, inner=True, outer=True):
        def plane(x, carry):
            at = pl.ds(x * hy if isinstance(x, int) else pl.multiple_of(x * hy, hy), hy)
            values = pad[pl.ds(first, ch), at]
            for b in range(3):
                for c in range(3):
                    step = (b - 1) * width + (c - 1)
                    moved = values
                    if step:
                        moved = pltpu.roll(values, (-step) % hy, 1)
                        fits = ((row_h + (b - 1) >= 0) & (row_h + (b - 1) < BLK)
                                & (row_y + (c - 1) >= 0) & (row_y + (c - 1) < width))
                        moved = jnp.where(fits, moved, jnp.zeros_like(moved))
                    out[pl.ds((3 * b + c) * ch, ch), at] = moved.astype(BF16)
            return carry
        if inner:
            lax.fori_loop(1, nx + 1, plane, 0, unroll=True)
        if outer:
            plane(0, 0)
            plane(nx + 1, 0)

    def conv(weight, stack):
        grown = jnp.dot(weight[...], stack[...], preferred_element_type=F32)
        return (grown[:ch, :flat] + grown[ch:2 * ch, hy:hy + flat]
                + grown[2 * ch:, 2 * hy:2 * hy + flat])

    nt = (((1,), (1,)), ((), ()))
    used = 27 * ch // 2

    def grad_by_input(stack, g):
        rows = 9 * ch
        side = rows // 2
        part[g, pl.ds(0, rows), :] = lax.dot_general(
            stack[...], d3[pl.ds(0, 2 * ch), :], nt, preferred_element_type=F32)
        rest = lax.dot_general(
            stack[...], d3[pl.ds(2 * ch, ch), :], nt, preferred_element_type=F32)
        part[g, pl.ds(rows, side), :] = jnp.concatenate([rest[:side], rest[side:]], axis=1)

    def grad_by_output(stack, g):
        rows = 3 * ch
        side = rows // 2
        for m in range(4):
            part[g, pl.ds(m * rows, rows), :] = lax.dot_general(
                d3[...], stack[pl.ds(m * 2 * ch, 2 * ch), :], nt, preferred_element_type=F32)
        rest = lax.dot_general(
            d3[...], stack[pl.ds(8 * ch, ch), :], nt, preferred_element_type=F32)
        part[g, pl.ds(4 * rows, side), :] = jnp.concatenate([rest[:side], rest[side:]], axis=1)

    def put_d3(value):
        for a in range(3):
            d3[pl.ds(a * ch, ch), pl.ds(a * hy, flat)] = value

    def to_rows(columns):
        spot = lax.broadcasted_iota(jnp.int32, (ch, LANES), 1)
        block = jnp.zeros((ch, LANES), F32)
        for index, column in enumerate(columns):
            block = jnp.where(spot == index, column, block)
        return jnp.transpose(block)[:8]

    def to_columns(rows):
        return jnp.transpose(jnp.concatenate([rows, jnp.zeros((LANES - 8, ch), F32)], axis=0))

    def small_start(call, first, second, third):
        ar[call, me, 0:1, :] = jnp.concatenate([first, second], axis=1)
        ar[call, me, 1:2, :] = jnp.concatenate([third, third], axis=1)
        each(n_all, lambda k: pltpu.make_async_remote_copy(
            src_ref=ar.at[call, me], dst_ref=ar.at[call, me],
            send_sem=ar_s.at[call], recv_sem=ar_r.at[call],
            device_id=peer(k), device_id_type=MESH).start())

    def small_end(call):
        arrived = ar.at[call, pl.ds(0, n_all - 1)]
        pltpu.make_async_copy(arrived, arrived, ar_r.at[call]).wait()
        pltpu.make_async_copy(arrived, arrived, ar_s.at[call]).wait()
        return ar[call, :, 0, :], ar[call, :, 1, :]

    def merge_moments(sums_squares, counts):
        total = jnp.sum(sums_squares, axis=0, keepdims=True)
        count = jnp.sum(counts, axis=0, keepdims=True)
        off = (sums_squares / jnp.maximum(counts, 1.0) - total / jnp.maximum(count, 1.0))
        between = jnp.sum(counts * off * off, axis=0, keepdims=True)
        return jnp.concatenate(
            [total[:, :ch], total[:, ch:] + between[:, :ch], count[:, :ch],
             jnp.zeros((5, ch), F32)], axis=0)

    def scatter_core(g):
        theirs = pl.ds(pl.multiple_of((1 - core) * rows_half, rows_half), rows_half)
        copy = pltpu.make_async_remote_copy(
            src_ref=part.at[g, theirs, :], dst_ref=rp.at[g],
            send_sem=rs_s.at[g, 0], recv_sem=rs_r.at[g, 0],
            device_id=sibling, device_id_type=MESH)
        copy.start()
        return copy

    def settle(g, stage, ref):
        pltpu.make_async_copy(ref, ref, rs_r.at[g, stage]).wait()

    def drain(g, stage, ref):
        pltpu.make_async_copy(ref, ref, rs_s.at[g, stage]).wait()

    def scatter_chips(g, copy):
        copy.wait()
        mine = pl.ds(pl.multiple_of(core * rows_half, rows_half), rows_half)
        total = part[g, mine, :] + rp[g]
        rp[g] = total
        half[g] = total.astype(BF16)

        def send(k):
            other, device = chip_peer(k)

            @pl.when(other < owners)
            def _():
                pltpu.make_async_remote_copy(
                    src_ref=half.at[g, pl.ds(pl.multiple_of(other * size, size), size), :],
                    dst_ref=r1.at[g, k - 1],
                    send_sem=rs_s.at[g, 1], recv_sem=rs_r.at[g, 1],
                    device_id=device, device_id_type=MESH).start()

        each(n_chips, send)

    def gather_chips(g):
        @pl.when(chip < owners)
        def _():
            settle(g, 1, r1.at[g])
            total = rp[g, pl.ds(pl.multiple_of(chip * size, size), size), :]
            for k in range(n_chips - 1):
                total = total + r1[g, k].astype(F32)
            place = pl.ds(pl.multiple_of(core * rows_half + chip * size, size), size)
            q4[g, place, :] = total.astype(BF16)

            def send(k):
                _, device = chip_peer(k)
                pltpu.make_async_remote_copy(
                    src_ref=q4.at[g, place, :], dst_ref=q4.at[g, place, :],
                    send_sem=rs_s.at[g, 2], recv_sem=rs_r.at[g, 2],
                    device_id=device, device_id_type=MESH).start()

            each(n_chips, send)

    def gather_core(g):
        @pl.when(chip < owners)
        def _():
            settle(g, 2, half.at[g, pl.ds(0, (owners - 1) * size), :])
            drain(g, 1, half.at[g, pl.ds(0, (owners - 1) * size), :])
            drain(g, 2, r1.at[g])

        @pl.when(chip >= owners)
        def _():
            settle(g, 2, half.at[g])
            drain(g, 1, half.at[g])

        mine = pl.ds(pl.multiple_of(core * rows_half, rows_half), rows_half)
        copy = pltpu.make_async_remote_copy(
            src_ref=q4.at[g, mine, :], dst_ref=q4.at[g, mine, :],
            send_sem=rs_s.at[g, 3], recv_sem=rs_r.at[g, 3],
            device_id=sibling, device_id_type=MESH)
        copy.start()
        return copy

    end_xd = halo(0, xd_pad, hy, xd_pad)
    shifts(xd_pad, 0, s_x, outer=False)
    zero_ends(xd_pad)
    zero_ends(a_pad)
    zero_ends(i_pad)
    end_xd()

    shifts(xd_pad, 0, s_x, inner=False)
    pre = conv(w1_ref, s_x)
    count_here = jnp.sum(mask, axis=1, keepdims=True)
    sums_here = jnp.sum(pre * mask, axis=1, keepdims=True)
    off = (pre - sums_here / jnp.maximum(count_here, 1.0)) * mask
    squares_here = jnp.sum(off * off, axis=1, keepdims=True)
    rows = to_rows([sums_here, squares_here])
    small_start(0, rows[0:1], rows[1:2], jnp.broadcast_to(count_here, (1, ch)))

    shifts(xd_pad, ch, s_d)
    as_flipped(k2_ref, w2f_ref)
    act_grad = conv(w2f_ref, s_d)
    gain_shift = to_columns(jnp.concatenate(
        [gain_ref[...], shift_ref[...], jnp.zeros((6, ch), F32)], axis=0))
    d3[...] = jnp.zeros(d3.shape, d3.dtype)
    if part.shape[1] > used:
        for g in range(2):
            part[g, pl.ds(used, part.shape[1] - used), :] = jnp.zeros(
                (part.shape[1] - used, LANES), F32)
    as_matrix(k2_ref, w2_ref)
    as_flipped(k1_ref, w1f_ref)

    moments = to_columns(merge_moments(*small_end(0)))
    count = moments[:, 2:3]
    mean = moments[:, 0:1] / count
    inv_std = lax.rsqrt(moments[:, 1:2] / count + EPSILON)
    gain, shift = gain_shift[:, 0:1], gain_shift[:, 1:2]
    normal = (pre - mean) * inv_std
    pre_act = gain * normal + shift
    sg = 1.0 / (1.0 + jnp.exp(-pre_act))
    act = (pre_act * sg * mask).astype(BF16)
    a_pad[:, pl.ds(hy, flat)] = act
    end_act = halo(1, a_pad, hy, a_pad)
    z_grad = act_grad * mask * sg * (1.0 + pre_act * (1.0 - sg))
    shift_here = jnp.sum(z_grad, axis=1, keepdims=True)
    gain_here = jnp.sum(z_grad * normal, axis=1, keepdims=True)
    rows = to_rows([shift_here, gain_here])
    small_start(1, rows[0:1], rows[1:2], rows[0:1])

    put_d3(act)
    grad_by_output(s_d, 0)
    two = scatter_core(0)
    shifts(a_pad, 0, s_t, outer=False)
    scatter_chips(0, two)
    end_act()
    shifts(a_pad, 0, s_t, inner=False)
    pre_two = conv(w2_ref, s_t)
    so_ref[...] = ((xd_pad[pl.ds(0, ch), pl.ds(hy, flat)].astype(F32) + pre_two) * mask).astype(BF16)

    totals = jnp.sum(small_end(1)[0], axis=0, keepdims=True)
    totals = jnp.concatenate([totals[:, :ch], totals[:, ch:], jnp.zeros((6, ch), F32)], axis=0)
    sums_out[...] = totals
    totals = to_columns(totals)
    delta_one = (gain * inv_std * (
        z_grad - totals[:, 0:1] / count - normal * (totals[:, 1:2] / count)) * mask).astype(BF16)
    i_pad[:, pl.ds(hy, flat)] = delta_one
    end_delta = halo(2, i_pad, hy, i_pad)
    put_d3(delta_one)
    grad_by_input(s_x, 1)
    one = scatter_core(1)
    gather_chips(0)
    scatter_chips(1, one)
    shifts(i_pad, 0, s_t, outer=False)
    end_delta()
    shifts(i_pad, 0, s_t, inner=False)
    back = conv(w1f_ref, s_t)
    ig_ref[...] = ((xd_pad[pl.ds(ch, ch), pl.ds(hy, flat)].astype(F32) + back) * mask).astype(BF16)
    two = gather_core(0)
    gather_chips(1)
    one = gather_core(1)
    two.wait()
    one.wait()


def unpack(ch, so_in, ig_in, q4, sums, so_ref, ig_ref, g1_ref, g2_ref, gain_ref, shift_ref):
    rows = 9 * ch
    half = rows // 2
    for a in range(2):
        g1_ref[pl.ds(a * rows, rows), :] = q4[1, pl.ds(0, rows), pl.ds(a * ch, ch)].astype(F32)
    for side in range(2):
        g1_ref[pl.ds(2 * rows + side * half, half), :] = (
            q4[1, pl.ds(rows, half), pl.ds(side * ch, ch)].astype(F32))
    rows = 3 * ch
    half = rows // 2
    for a in range(3):
        for m in range(4):
            for side in range(2):
                g2_ref[pl.ds((26 - 9 * a - 2 * m - side) * ch, ch), :] = (
                    q4[0, pl.ds(m * rows + a * ch, ch), pl.ds(side * ch, ch)].astype(F32))
    step = ch // 2
    for part in range(6):
        side, row = part // 3, part % 3
        a, top = part // 2, part % 2
        g2_ref[pl.ds((18 - 9 * a) * ch + top * step, step), :] = (
            q4[0, pl.ds(4 * rows + row * step, step), pl.ds(side * ch, ch)].astype(F32))
    so_ref[...] = so_in[...]
    ig_ref[...] = ig_in[...]
    shift_ref[...] = sums[0:1, :]
    gain_ref[...] = sums[1:2, :]


def local(n_dp, n_tile, features, occupied, conv_one, conv_two, gain, shift, cotangent):
    scenes, ch, nx, hy = features.shape
    flat = nx * hy
    xd = jnp.concatenate([features.reshape(ch, flat), cotangent.reshape(ch, flat)], axis=0)
    n_chips, n_all = n_dp * n_tile // 2, n_dp * n_tile
    used = 27 * ch // 2
    size = -(-used // (2 * n_chips * 16)) * 16
    rows_half = -(-used // (2 * size)) * size
    rows = 2 * rows_half
    vmem = pl.BlockSpec(memory_space=pltpu.VMEM)
    dma = pltpu.SemaphoreType.DMA
    so, ig, q4, sums = pl.pallas_call(
        functools.partial(kernel, n_dp, n_tile, ch, nx, hy),
        out_shape=(
            jax.ShapeDtypeStruct((ch, flat), BF16),
            jax.ShapeDtypeStruct((ch, flat), BF16),
            jax.ShapeDtypeStruct((2, rows, LANES), BF16),
            jax.ShapeDtypeStruct((8, ch), F32),
        ),
        in_specs=[vmem, pl.BlockSpec(memory_space=pltpu.SMEM)] + [vmem] * 4,
        out_specs=[vmem] * 4,
        scratch_shapes=[
            pltpu.VMEM((3 * ch, 9 * ch), BF16),
            pltpu.VMEM((3 * ch, 9 * ch), BF16),
            pltpu.VMEM((3 * ch, 9 * ch), BF16),
            pltpu.VMEM((3 * ch, 9 * ch), BF16),
            pltpu.VMEM((2 * ch, flat + 2 * hy), BF16),
            pltpu.VMEM((ch, flat + 2 * hy), BF16),
            pltpu.VMEM((ch, flat + 2 * hy), BF16),
            pltpu.VMEM((9 * ch, flat + 2 * hy), BF16),
            pltpu.VMEM((9 * ch, flat + 2 * hy), BF16),
            pltpu.VMEM((9 * ch, flat + 2 * hy), BF16),
            pltpu.VMEM((3 * ch, flat + 2 * hy), BF16),
            pltpu.VMEM((2, n_all, 2, LANES), F32),
            pltpu.VMEM((2, rows, LANES), F32),
            pltpu.VMEM((2, rows_half, LANES), F32),
            pltpu.VMEM((2, rows_half, LANES), BF16),
            pltpu.VMEM((2, n_chips - 1, size, LANES), BF16),
            dma((3, 2)), dma((3, 2)),
            dma((2,)), dma((2,)),
            dma((2, 4)), dma((2, 4)),
        ],
        compiler_params=pltpu.CompilerParams(
            collective_id=0, has_side_effects=True, vmem_limit_bytes=48 * 2**20),
    )(
        xd, occupied[0], conv_one.reshape(27 * ch, ch), conv_two.reshape(27 * ch, ch),
        gain.reshape(1, ch), shift.reshape(1, ch),
    )
    planes = features.shape[1:]
    so, ig, g1, g2, gg, sg = pl.pallas_call(
        functools.partial(unpack, ch),
        out_shape=(
            jax.ShapeDtypeStruct(planes, BF16),
            jax.ShapeDtypeStruct(planes, BF16),
            jax.ShapeDtypeStruct((27 * ch, ch), F32),
            jax.ShapeDtypeStruct((27 * ch, ch), F32),
            jax.ShapeDtypeStruct((1, ch), F32),
            jax.ShapeDtypeStruct((1, ch), F32),
        ),
        in_specs=[vmem] * 4,
        out_specs=[vmem] * 6,
        compiler_params=pltpu.CompilerParams(vmem_limit_bytes=16 * 2**20),
    )(so.reshape(planes), ig.reshape(planes), q4, sums)
    shape = features.shape
    return (so.reshape(shape), ig.reshape(shape), g1.reshape(27, ch, ch),
            g2.reshape(27, ch, ch), gg.reshape(ch), sg.reshape(ch))


def solution(mesh):
    split = P("dp", None, "tile", None)
    return jax.shard_map(
        functools.partial(local, mesh.shape["dp"], mesh.shape["tile"]),
        mesh=mesh,
        in_specs=(split, P("dp", "tile", None), P(), P(), P(), P(), split),
        out_specs=(split, split, P(), P(), P(), P()),
        check_vma=False,
    )
```

time: 48.2 us -> 40.4 us (0.84)
  Pallas kernels: 45.5 us -> 37.7 us
    pallas_call x1, Pallas kernels: 44.1 us -> 36.3 us  [local(): pl.pallas_call(functools.partial(kernel, n_dp, n_tile, ch, nx, hy), out_s...]
where the time goes in v1:
time: 40.4 us; the launch traced here: 40.2 us
  Pallas kernels  37.7 us (93%)
  local copies, waits for them, and re-layouts  1.78 us (4%)
  between operations  0.72 us (2%)
    pallas_call x1, Pallas kernels, local(): pl.pallas_call(functools.partial(kernel, n_dp, n_tile, ch, nx, hy), out_s...  36.3 us
    pallas_call x1, Pallas kernels, local(): pl.pallas_call(functools.partial(unpack, ch), out_shape=(jax.ShapeDtypeSt...  1.42 us
    reshape x1, local copies, waits for them, and re-layouts, local(): cotangent.reshape(ch, flat)  1.07 us

profile of v1, /device:TPU:0, one launch (start us, length us, event | category | flops | bytes accessed | tf_op | source)
XLA Modules:
  0.0 40.2 jit_solution(11036673962113779076)
XLA Ops:
  0.6 0.0 copy-start
  0.6 0.0 copy-start.1
  0.7 1.1 %copy_bitcast_fusion = (bf16[64,1024]{1,0:T(8,128)(2,1)S(1)}, bf16[64,1024]{1,0:T(8,128)(2,1)S(1)}) fusion(bf16[8,8,8,128]{3,2,1,0:T(8,128)(2,1)} %bitcast.32, bf16[8,8,8,128]{3,2,1,0:T(8,128)(2,1)} %bitcast.33), kind=kLoop, calls=%fused_computation.1 | loop fusion | bytes 524288 | tf_op jit(solution)/shard_map/reshape | solution.py:398
  1.7 0.0 copy-start.2
  1.7 0.0 copy-start.3
  1.8 0.0 copy-start.4
  1.8 0.0 copy-done
  1.8 0.1 copy-done.1
  1.9 0.5 %copy-done.2 = s32[1,1,2]{2,1,0:T(1,128)S(1)} copy-done((s32[1,1,2]{2,1,0:T(1,128)S(1)}, s32[1,1,2]{2,1,0:T(1,128)}, u32[]{:S(2)}) %copy-start.2) | copy-done | bytes 32
  2.4 0.0 copy-done.3
  2.4 0.0 copy-done.4
  2.5 36.3 %shard_map.118 = (bf16[64,1024]{1,0:T(8,128)(2,1)S(1)}, bf16[64,1024]{1,0:T(8,128)(2,1)S(1)}, bf16[2,896,128]{2,1,0:T(8,128)(2,1)S(1)}, f32[8,64]{1,0:T(8,128)S(1)}) custom-call(bf16[128,1024]{1,0:T(8,128)(2,1)S(1)} %pad_maximum_fusion.xd_ref, s32[1,2]{1,0:T(1,128)S(1)} %bitcast.29, bf16[1728,64]{1,0:T(8,128)(2,1)S(1)} %bitcast.25, ...), custom_call_target="tpu_custom_call" | custom-call | tf_op jit(solution)/shard_map/pallas_call | solution.py:406
  38.8 1.4 %shard_map.119 = (bf16[64,8,128]{2,1,0:T(8,128)(2,1)}, bf16[64,8,128]{2,1,0:T(8,128)(2,1)}, f32[1728,64]{1,0:T(8,128)}, f32[1728,64]{1,0:T(8,128)}, f32[1,64]{1,0:T(1,128)}, /*index=5*/f32[1,64]{1,0:T(1,128)}) custom-call(bf16[64,8,128]{2,1,0:T(8,128)(2,1)S(1)} %bitcast.23, bf16[64,8,128]{2,1,0:T(8,128)(2,1)S(1)} %bitcast.24, ...), custom_call_target="tpu_custom_call" | custom-call | tf_op jit(solution)/shard_map/pallas_call | solution.py:444
  (3 shorter events, 0.1 us)
Async XLA Ops:
  0.6 1.2 %copy-start = (bf16[27,64,64]{2,1,0:T(8,128)(2,1)S(1)}, bf16[27,64,64]{2,1,0:T(8,128)(2,1)}, u32[]{:S(2)}) copy-start(bf16[27,64,64]{2,1,0:T(8,128)(2,1)} %param.9) | copy-start | bytes 663556
  0.6 1.3 %copy-start.1 = (bf16[27,64,64]{2,1,0:T(8,128)(2,1)S(1)}, bf16[27,64,64]{2,1,0:T(8,128)(2,1)}, u32[]{:S(2)}) copy-start(bf16[27,64,64]{2,1,0:T(8,128)(2,1)} %param.10) | copy-start | bytes 663556
  1.7 0.7 %copy-start.2 = (s32[1,1,2]{2,1,0:T(1,128)S(1)}, s32[1,1,2]{2,1,0:T(1,128)}, u32[]{:S(2)}) copy-start(s32[1,1,2]{2,1,0:T(1,128)} %param.8) | copy-start | bytes 28
  1.7 0.7 %copy-start.3 = (f32[64]{0:T(128)S(1)}, f32[64]{0:T(128)}, u32[]{:S(2)}) copy-start(f32[64]{0:T(128)} %param.11) | copy-start | bytes 772
  1.8 0.7 %copy-start.4 = (f32[64]{0:T(128)S(1)}, f32[64]{0:T(128)}, u32[]{:S(2)}) copy-start(f32[64]{0:T(128)} %param.12) | copy-start | bytes 772

commit v2 on v1

--- a/solution.py
+++ b/solution.py
@@ -17,8 +17,9 @@
 
 def kernel(
     n_dp, n_tile, ch, nx, hy,
-    xd_ref, occ_ref, k1_ref, k2_ref, gain_ref, shift_ref,
+    x_hbm, d_hbm, occ_hbm, k1_hbm, k2_hbm, gain_hbm, shift_hbm,
     so_ref, ig_ref, q4, sums_out,
+    occ_ref, k1_ref, k2_ref, gain_ref, shift_ref, raw, tall, in_sem,
     w1_ref, w2_ref, w1f_ref, w2f_ref, xd_pad, a_pad, i_pad, s_x, s_d, s_t, d3, ar, part, rp, half, r1,
     halo_s, halo_r, ar_s, ar_r, rs_s, rs_r,
 ):
@@ -53,15 +54,29 @@
     each(n_all, lambda k: pl.semaphore_signal(
         barrier, inc=1, device_id=peer(k), device_id_type=MESH))
 
+    loads = [pltpu.make_async_copy(src, dst, in_sem.at[i]) for i, (src, dst) in enumerate((
+        (occ_hbm, occ_ref), (x_hbm, raw.at[0]), (d_hbm, raw.at[1]), (k1_hbm, k1_ref),
+        (k2_hbm, k2_ref), (gain_hbm, gain_ref), (shift_hbm, shift_ref)))]
+    for load in loads:
+        load.start()
+
     width = hy // BLK
     spot = lax.broadcasted_iota(jnp.int32, (1, flat), 1)
     block_x, block_y = spot // (hy * BLK), lax.rem(spot, width) // BLK
     mask = jnp.zeros((1, flat), F32)
+    loads[0].wait()
     for bx in range(nx // BLK):
         for by in range(width // BLK):
             mask = jnp.where((block_x == bx) & (block_y == by),
                              occ_ref[bx, by].astype(F32), mask)
-    xd_pad[:, pl.ds(hy, flat)] = (xd_ref[...].astype(F32) * mask).astype(BF16)
+    for i in range(2):
+        loads[1 + i].wait()
+        tall[i] = raw[i].astype(F32).reshape(ch * nx, hy)
+        for x in range(nx):
+            xd_pad[pl.ds(i * ch, ch), pl.ds((x + 1) * hy, hy)] = (
+                tall[i, pl.ds(x, ch, stride=nx), :] * mask[:, x * hy:(x + 1) * hy]).astype(BF16)
+    for load in loads[3:]:
+        load.wait()
     same = (lax.broadcasted_iota(jnp.int32, (ch, ch), 0)
             == lax.broadcasted_iota(jnp.int32, (ch, ch), 1)).astype(BF16)
 
@@ -321,15 +336,15 @@
     normal = (pre - mean) * inv_std
     pre_act = gain * normal + shift
     sg = 1.0 / (1.0 + jnp.exp(-pre_act))
-    act = (pre_act * sg * mask).astype(BF16)
-    a_pad[:, pl.ds(hy, flat)] = act
-    end_act = halo(1, a_pad, hy, a_pad)
     z_grad = act_grad * mask * sg * (1.0 + pre_act * (1.0 - sg))
     shift_here = jnp.sum(z_grad, axis=1, keepdims=True)
     gain_here = jnp.sum(z_grad * normal, axis=1, keepdims=True)
     rows = to_rows([shift_here, gain_here])
     small_start(1, rows[0:1], rows[1:2], rows[0:1])
 
+    act = (pre_act * sg * mask).astype(BF16)
+    a_pad[:, pl.ds(hy, flat)] = act
+    end_act = halo(1, a_pad, hy, a_pad)
     put_d3(act)
     grad_by_output(s_d, 0)
     two = scatter_core(0)
@@ -395,7 +410,6 @@
 def local(n_dp, n_tile, features, occupied, conv_one, conv_two, gain, shift, cotangent):
     scenes, ch, nx, hy = features.shape
     flat = nx * hy
-    xd = jnp.concatenate([features.reshape(ch, flat), cotangent.reshape(ch, flat)], axis=0)
     n_chips, n_all = n_dp * n_tile // 2, n_dp * n_tile
     used = 27 * ch // 2
     size = -(-used // (2 * n_chips * 16)) * 16
@@ -411,9 +425,17 @@
             jax.ShapeDtypeStruct((2, rows, LANES), BF16),
             jax.ShapeDtypeStruct((8, ch), F32),
         ),
-        in_specs=[vmem, pl.BlockSpec(memory_space=pltpu.SMEM)] + [vmem] * 4,
+        in_specs=[pl.BlockSpec(memory_space=pltpu.HBM)] * 7,
         out_specs=[vmem] * 4,
         scratch_shapes=[
+            pltpu.SMEM(occupied.shape[1:], jnp.int32),
+            pltpu.VMEM((27 * ch, ch), BF16),
+            pltpu.VMEM((27 * ch, ch), BF16),
+            pltpu.VMEM((1, ch), F32),
+            pltpu.VMEM((1, ch), F32),
+            pltpu.VMEM((2, ch, nx, hy), BF16),
+            pltpu.VMEM((2, ch * nx, hy), F32),
+            dma((7,)),
             pltpu.VMEM((3 * ch, 9 * ch), BF16),
             pltpu.VMEM((3 * ch, 9 * ch), BF16),
             pltpu.VMEM((3 * ch, 9 * ch), BF16),
@@ -437,9 +459,9 @@
         compiler_params=pltpu.CompilerParams(
             collective_id=0, has_side_effects=True, vmem_limit_bytes=48 * 2**20),
     )(
-        xd, occupied[0], conv_one.reshape(27 * ch, ch), conv_two.reshape(27 * ch, ch),
-        gain.reshape(1, ch), shift.reshape(1, ch),
-    )
+        *(pltpu.with_memory_space_constraint(value, pltpu.HBM) for value in (
+            features[0], cotangent[0], occupied[0], conv_one.reshape(27 * ch, ch),
+            conv_two.reshape(27 * ch, ch), gain.reshape(1, ch), shift.reshape(1, ch))))
     planes = features.shape[1:]
     so, ig, g1, g2, gg, sg = pl.pallas_call(
         functools.partial(unpack, ch),

time: 40.4 us -> 37.9 us (0.938)
  local copies, waits for them, and re-layouts: 1.78 us -> 0.04 us
  Pallas kernels: 37.7 us -> 37.1 us
    reshape x1 -> x0, local copies, waits for them, and re-layouts: 1.07 us -> none  [local(): cotangent.reshape(ch, flat)]
    unnamed x12 -> x2, local copies, waits for them, and re-layouts: 0.71 us -> 0.04 us
    pallas_call x1, Pallas kernels: 36.3 us -> 35.7 us  [local(): pl.pallas_call(functools.partial(kernel, n_dp, n_tile, ch, nx, hy), out_s...]
where the time goes in v2:
time: 37.9 us; the launch traced here: 37.8 us
  Pallas kernels  37.1 us (98%)
  between operations  0.66 us (2%)
    pallas_call x1, Pallas kernels, local(): pl.pallas_call(functools.partial(kernel, n_dp, n_tile, ch, nx, hy), out_s...  35.7 us
    pallas_call x1, Pallas kernels, local(): pl.pallas_call(functools.partial(unpack, ch), out_shape=(jax.ShapeDtypeSt...  1.42 us

profile of v2, /device:TPU:0, one launch (start us, length us, event | category | flops | bytes accessed | tf_op | source)
XLA Modules:
  0.0 37.8 jit_solution(4894724280663756333)
XLA Ops:
  0.6 35.7 %shard_map.118 = (bf16[64,1024]{1,0:T(8,128)(2,1)S(1)}, bf16[64,1024]{1,0:T(8,128)(2,1)S(1)}, bf16[2,896,128]{2,1,0:T(8,128)(2,1)S(1)}, f32[8,64]{1,0:T(8,128)S(1)}) custom-call(bf16[64,8,128]{2,1,0:T(8,128)(2,1)} %bitcast.23, bf16[64,8,128]{2,1,0:T(8,128)(2,1)} %bitcast.24, s32[1,2]{1,0:T(1,128)} %bitcast.25, bf16[1728,64]{1,0:T(8,128)(2,1)} %bitcast.21, ...), custom_call_target="tpu_custom_call" | custom-call | tf_op jit(solution)/shard_map/pallas_call | solution.py:420
  36.4 1.4 %shard_map.119 = (bf16[64,8,128]{2,1,0:T(8,128)(2,1)}, bf16[64,8,128]{2,1,0:T(8,128)(2,1)}, f32[1728,64]{1,0:T(8,128)}, f32[1728,64]{1,0:T(8,128)}, f32[1,64]{1,0:T(1,128)}, /*index=5*/f32[1,64]{1,0:T(1,128)}) custom-call(bf16[64,8,128]{2,1,0:T(8,128)(2,1)S(1)} %bitcast.17, bf16[64,8,128]{2,1,0:T(8,128)(2,1)S(1)} %bitcast.18, ...), custom_call_target="tpu_custom_call" | custom-call | tf_op jit(solution)/shard_map/pallas_call | solution.py:466
  (2 shorter events, 0.0 us)

commit v3 on v2

--- a/solution.py
+++ b/solution.py
@@ -29,9 +29,12 @@
     core, z = lax.rem(tile, 2), tile // 2
     me, chip = dp * n_tile + tile, dp * n_z + z
     flat = nx * hy
-    rows_half = half.shape[1]
     size = r1.shape[2]
-    owners = rows_half // size
+    group = n_z * size
+    used = 27 * ch // 2
+    blocks = -(-used // size)
+    rows_core = (n_chips * size, -(-used // (2 * size)) * size)
+    owners = ((min(blocks, n_chips), blocks - min(blocks, n_chips)), (rows_core[1] // size,) * 2)
 
     def each(count, body):
         def step(k, carry):
@@ -167,26 +170,28 @@
                 + grown[2 * ch:, 2 * hy:2 * hy + flat])
 
     nt = (((1,), (1,)), ((), ()))
-    used = 27 * ch // 2
-
-    def grad_by_input(stack, g):
-        rows = 9 * ch
-        side = rows // 2
-        part[g, pl.ds(0, rows), :] = lax.dot_general(
-            stack[...], d3[pl.ds(0, 2 * ch), :], nt, preferred_element_type=F32)
-        rest = lax.dot_general(
-            stack[...], d3[pl.ds(2 * ch, ch), :], nt, preferred_element_type=F32)
-        part[g, pl.ds(rows, side), :] = jnp.concatenate([rest[:side], rest[side:]], axis=1)
+
+    def grad_by_input(stack, g, which):
+        count = 9 * ch // 2
+        side = count // 2
+        first = which * rows_core[g]
+        found = lax.dot_general(
+            stack[span(which * count, count, 16), :], d3[...], nt, preferred_element_type=F32)
+        part[g, span(first, count, 8), :] = found[:, :2 * ch]
+        part[g, span(first + count, side, 8), :] = jnp.concatenate(
+            [found[:side, 2 * ch:], found[side:, 2 * ch:]], axis=1)
 
     def grad_by_output(stack, g):
         rows = 3 * ch
         side = rows // 2
+        found = lax.dot_general(d3[...], stack[...], nt, preferred_element_type=F32)
         for m in range(4):
-            part[g, pl.ds(m * rows, rows), :] = lax.dot_general(
-                d3[...], stack[pl.ds(m * 2 * ch, 2 * ch), :], nt, preferred_element_type=F32)
-        rest = lax.dot_general(
-            d3[...], stack[pl.ds(8 * ch, ch), :], nt, preferred_element_type=F32)
-        part[g, pl.ds(4 * rows, side), :] = jnp.concatenate([rest[:side], rest[side:]], axis=1)
+            part[g, pl.ds(m * rows, rows), :] = found[:, m * 2 * ch:(m + 1) * 2 * ch]
+        part[g, pl.ds(4 * rows, side), :] = jnp.concatenate(
+            [found[:side, 8 * ch:], found[side:, 8 * ch:]], axis=1)
+
+    def span(start, count, step):
+        return pl.ds(pl.multiple_of(start, step), count)
 
     def put_d3(value):
         for a in range(3):
@@ -225,14 +230,11 @@
             [total[:, :ch], total[:, ch:] + between[:, :ch], count[:, :ch],
              jnp.zeros((5, ch), F32)], axis=0)
 
-    def scatter_core(g):
-        theirs = pl.ds(pl.multiple_of((1 - core) * rows_half, rows_half), rows_half)
-        copy = pltpu.make_async_remote_copy(
-            src_ref=part.at[g, theirs, :], dst_ref=rp.at[g],
-            send_sem=rs_s.at[g, 0], recv_sem=rs_r.at[g, 0],
-            device_id=sibling, device_id_type=MESH)
-        copy.start()
-        return copy
+    def by_core(g, body):
+        for side in range(2):
+            count = owners[g][side]
+            pl.when((core == side) & (chip < count))(lambda: body(True, count))
+            pl.when((core == side) & (chip >= count))(lambda: body(False, count))
 
     def settle(g, stage, ref):
         pltpu.make_async_copy(ref, ref, rs_r.at[g, stage]).wait()
@@ -240,74 +242,122 @@
     def drain(g, stage, ref):
         pltpu.make_async_copy(ref, ref, rs_s.at[g, stage]).wait()
 
-    def scatter_chips(g, copy):
-        copy.wait()
-        mine = pl.ds(pl.multiple_of(core * rows_half, rows_half), rows_half)
-        total = part[g, mine, :] + rp[g]
-        rp[g] = total
-        half[g] = total.astype(BF16)
-
-        def send(k):
+    def send(g, stage, src, dst, device):
+        pltpu.make_async_remote_copy(
+            src_ref=src, dst_ref=dst, send_sem=rs_s.at[g, stage], recv_sem=rs_r.at[g, stage],
+            device_id=device, device_id_type=MESH).start()
+
+    def scatter_core(g):
+        rows = rows_core[g]
+        send(g, 0, part.at[g, span((1 - core) * rows, rows, size), :], rp.at[g, pl.ds(0, rows), :],
+             sibling)
+
+    def add_core(g):
+        rows = rows_core[g]
+        done = rp.at[g, pl.ds(0, rows), :]
+        settle(g, 0, done)
+        drain(g, 0, done)
+        total = part[g, span(core * rows, rows, size), :] + rp[g, pl.ds(0, rows), :]
+        rp[g, pl.ds(0, rows), :] = total
+        return total
+
+    def scatter_chips(g):
+        half[g, pl.ds(0, rows_core[g]), :] = add_core(g).astype(BF16)
+        here = jnp.where(core == 0, owners[g][0], owners[g][1])
+
+        def step(k):
             other, device = chip_peer(k)
 
-            @pl.when(other < owners)
+            @pl.when(other < here)
             def _():
-                pltpu.make_async_remote_copy(
-                    src_ref=half.at[g, pl.ds(pl.multiple_of(other * size, size), size), :],
-                    dst_ref=r1.at[g, k - 1],
-                    send_sem=rs_s.at[g, 1], recv_sem=rs_r.at[g, 1],
-                    device_id=device, device_id_type=MESH).start()
-
-        each(n_chips, send)
-
-    def gather_chips(g):
-        @pl.when(chip < owners)
-        def _():
+                send(g, 1, half.at[g, span(other * size, size, size), :], r1.at[g, k - 1], device)
+
+        each(n_chips, step)
+
+    def sum_chips(g, owned):
+        place = q4.at[g, span(core * rows_core[g] + chip * size, size, size), :]
+        if owned:
             settle(g, 1, r1.at[g])
-            total = rp[g, pl.ds(pl.multiple_of(chip * size, size), size), :]
+            total = rp[g, span(chip * size, size, size), :]
             for k in range(n_chips - 1):
                 total = total + r1[g, k].astype(F32)
-            place = pl.ds(pl.multiple_of(core * rows_half + chip * size, size), size)
-            q4[g, place, :] = total.astype(BF16)
-
-            def send(k):
-                _, device = chip_peer(k)
-                pltpu.make_async_remote_copy(
-                    src_ref=q4.at[g, place, :], dst_ref=q4.at[g, place, :],
-                    send_sem=rs_s.at[g, 2], recv_sem=rs_r.at[g, 2],
-                    device_id=device, device_id_type=MESH).start()
-
-            each(n_chips, send)
+            place[...] = total.astype(BF16)
+        else:
+            place[...] = jnp.zeros((size, LANES), BF16)
+        return place
+
+    def drain_chips(g, owned, count):
+        if count > owned:
+            drain(g, 1, half.at[g, pl.ds(0, (count - owned) * size), :])
+
+    def gather_chips(g):
+        def body(owned, count):
+            if owned:
+                place = sum_chips(g, owned)
+                each(n_chips, lambda k: send(g, 2, place, place, chip_peer(k)[1]))
+        by_core(g, body)
 
     def gather_core(g):
-        @pl.when(chip < owners)
-        def _():
-            settle(g, 2, half.at[g, pl.ds(0, (owners - 1) * size), :])
-            drain(g, 1, half.at[g, pl.ds(0, (owners - 1) * size), :])
-            drain(g, 2, r1.at[g])
-
-        @pl.when(chip >= owners)
-        def _():
-            settle(g, 2, half.at[g])
-            drain(g, 1, half.at[g])
-
-        mine = pl.ds(pl.multiple_of(core * rows_half, rows_half), rows_half)
-        copy = pltpu.make_async_remote_copy(
-            src_ref=q4.at[g, mine, :], dst_ref=q4.at[g, mine, :],
-            send_sem=rs_s.at[g, 3], recv_sem=rs_r.at[g, 3],
-            device_id=sibling, device_id_type=MESH)
-        copy.start()
-        return copy
+        rows = rows_core[g]
+        mine = q4.at[g, span(core * rows, rows, size), :]
+        send(g, 3, mine, mine, sibling)
+
+    def end_core(g):
+        rows = q4.at[g, pl.ds(0, rows_core[g]), :]
+        settle(g, 3, rows)
+        drain(g, 3, rows)
+
+    def end_chips(g):
+        def body(owned, count):
+            drain_chips(g, owned, count)
+            settle(g, 2, half.at[g, pl.ds(0, (count - owned) * size), :])
+            if owned:
+                drain(g, 2, r1.at[g])
+        by_core(g, body)
+
+    def plane_peer(k):
+        other = lax.rem(dp + k, n_dp)
+        return other, (other, tile)
+
+    def line_peer(k):
+        other = lax.rem(z + k, n_z)
+        return other, (dp, other * 2 + core)
+
+    def gather_line(g):
+        def body(owned, count):
+            sum_chips(g, owned)
+            drain_chips(g, owned, count)
+        by_core(g, body)
+        place = q4.at[g, span(core * rows_core[g] + chip * size, size, size), :]
+        each(n_z, lambda k: send(g, 4, place, place, line_peer(k)[1]))
+
+    def gather_plane(g):
+        others = q4.at[g, pl.ds(0, (n_z - 1) * size), :]
+        settle(g, 4, others)
+        place = q4.at[g, span(core * rows_core[g] + dp * group, group, size), :]
+        each(n_dp, lambda k: send(g, 5, place, place, plane_peer(k)[1]))
+        drain(g, 4, others)
+
+    def end_plane(g):
+        others = q4.at[g, pl.ds(0, (n_dp - 1) * group), :]
+        settle(g, 5, others)
+        drain(g, 5, others)
 
     end_xd = halo(0, xd_pad, hy, xd_pad)
     shifts(xd_pad, 0, s_x, outer=False)
     zero_ends(xd_pad)
     zero_ends(a_pad)
     zero_ends(i_pad)
+    inside = jnp.dot(w1_ref[...], s_x[:, pl.ds(hy, flat)], preferred_element_type=F32)
     end_xd()
 
     shifts(xd_pad, 0, s_x, inner=False)
-    pre = conv(w1_ref, s_x)
+    before = jnp.dot(w1_ref[pl.ds(0, ch), :], s_x[:, pl.ds(0, hy)], preferred_element_type=F32)
+    after = jnp.dot(w1_ref[pl.ds(2 * ch, ch), :], s_x[:, pl.ds(hy + flat, hy)],
+                    preferred_element_type=F32)
+    pre = (inside[ch:2 * ch]
+           + jnp.concatenate([before, inside[:ch, :flat - hy]], axis=1)
+           + jnp.concatenate([inside[2 * ch:, hy:], after], axis=1))
     count_here = jnp.sum(mask, axis=1, keepdims=True)
     sums_here = jnp.sum(pre * mask, axis=1, keepdims=True)
     off = (pre - sums_here / jnp.maximum(count_here, 1.0)) * mask
@@ -321,10 +371,11 @@
     gain_shift = to_columns(jnp.concatenate(
         [gain_ref[...], shift_ref[...], jnp.zeros((6, ch), F32)], axis=0))
     d3[...] = jnp.zeros(d3.shape, d3.dtype)
-    if part.shape[1] > used:
-        for g in range(2):
-            part[g, pl.ds(used, part.shape[1] - used), :] = jnp.zeros(
-                (part.shape[1] - used, LANES), F32)
+    for g, (first, last) in ((0, (used, 2 * rows_core[0])),
+                             (1, (used // 2, rows_core[1])),
+                             (1, (rows_core[1] + used // 2, 2 * rows_core[1]))):
+        if last > first:
+            part[g, pl.ds(first, last - first), :] = jnp.zeros((last - first, LANES), F32)
     as_matrix(k2_ref, w2_ref)
     as_flipped(k1_ref, w1f_ref)
 
@@ -347,9 +398,9 @@
     end_act = halo(1, a_pad, hy, a_pad)
     put_d3(act)
     grad_by_output(s_d, 0)
-    two = scatter_core(0)
+    scatter_core(0)
     shifts(a_pad, 0, s_t, outer=False)
-    scatter_chips(0, two)
+    scatter_chips(0)
     end_act()
     shifts(a_pad, 0, s_t, inner=False)
     pre_two = conv(w2_ref, s_t)
@@ -364,30 +415,37 @@
     i_pad[:, pl.ds(hy, flat)] = delta_one
     end_delta = halo(2, i_pad, hy, i_pad)
     put_d3(delta_one)
-    grad_by_input(s_x, 1)
-    one = scatter_core(1)
-    gather_chips(0)
-    scatter_chips(1, one)
+    grad_by_input(s_x, 1, 1 - core)
+    scatter_core(1)
+    grad_by_input(s_x, 1, core)
+    gather_line(0)
+    scatter_chips(1)
     shifts(i_pad, 0, s_t, outer=False)
     end_delta()
     shifts(i_pad, 0, s_t, inner=False)
     back = conv(w1f_ref, s_t)
     ig_ref[...] = ((xd_pad[pl.ds(ch, ch), pl.ds(hy, flat)].astype(F32) + back) * mask).astype(BF16)
-    two = gather_core(0)
+    gather_plane(0)
     gather_chips(1)
-    one = gather_core(1)
-    two.wait()
-    one.wait()
-
-
-def unpack(ch, so_in, ig_in, q4, sums, so_ref, ig_ref, g1_ref, g2_ref, gain_ref, shift_ref):
-    rows = 9 * ch
-    half = rows // 2
-    for a in range(2):
-        g1_ref[pl.ds(a * rows, rows), :] = q4[1, pl.ds(0, rows), pl.ds(a * ch, ch)].astype(F32)
-    for side in range(2):
-        g1_ref[pl.ds(2 * rows + side * half, half), :] = (
-            q4[1, pl.ds(rows, half), pl.ds(side * ch, ch)].astype(F32))
+    end_plane(0)
+    gather_core(0)
+    end_chips(1)
+    gather_core(1)
+    end_core(0)
+    end_core(1)
+
+
+def unpack(ch, rows_core, so_in, ig_in, q4, sums, so_ref, ig_ref, g1_ref, g2_ref, gain_ref, shift_ref):
+    count = 9 * ch // 2
+    side = count // 2
+    for core in range(2):
+        first = core * rows_core
+        for a in range(2):
+            g1_ref[pl.ds(a * 9 * ch + core * count, count), :] = (
+                q4[1, pl.ds(first, count), pl.ds(a * ch, ch)].astype(F32))
+        for k in range(2):
+            g1_ref[pl.ds(18 * ch + core * count + k * side, side), :] = (
+                q4[1, pl.ds(first + count, side), pl.ds(k * ch, ch)].astype(F32))
     rows = 3 * ch
     half = rows // 2
     for a in range(3):
@@ -414,7 +472,7 @@
     used = 27 * ch // 2
     size = -(-used // (2 * n_chips * 16)) * 16
     rows_half = -(-used // (2 * size)) * size
-    rows = 2 * rows_half
+    rows = 2 * n_chips * size
     vmem = pl.BlockSpec(memory_space=pltpu.VMEM)
     dma = pltpu.SemaphoreType.DMA
     so, ig, q4, sums = pl.pallas_call(
@@ -449,12 +507,12 @@
             pltpu.VMEM((3 * ch, flat + 2 * hy), BF16),
             pltpu.VMEM((2, n_all, 2, LANES), F32),
             pltpu.VMEM((2, rows, LANES), F32),
-            pltpu.VMEM((2, rows_half, LANES), F32),
-            pltpu.VMEM((2, rows_half, LANES), BF16),
+            pltpu.VMEM((2, rows // 2, LANES), F32),
+            pltpu.VMEM((2, rows // 2, LANES), BF16),
             pltpu.VMEM((2, n_chips - 1, size, LANES), BF16),
             dma((3, 2)), dma((3, 2)),
             dma((2,)), dma((2,)),
-            dma((2, 4)), dma((2, 4)),
+            dma((2, 6)), dma((2, 6)),
         ],
         compiler_params=pltpu.CompilerParams(
             collective_id=0, has_side_effects=True, vmem_limit_bytes=48 * 2**20),
@@ -464,7 +522,7 @@
             conv_two.reshape(27 * ch, ch), gain.reshape(1, ch), shift.reshape(1, ch))))
     planes = features.shape[1:]
     so, ig, g1, g2, gg, sg = pl.pallas_call(
-        functools.partial(unpack, ch),
+        functools.partial(unpack, ch, rows_half),
         out_shape=(
             jax.ShapeDtypeStruct(planes, BF16),
             jax.ShapeDtypeStruct(planes, BF16),

time: 37.9 us -> 35.8 us (0.945)
  Pallas kernels: 37.1 us -> 34.9 us
    pallas_call x1, Pallas kernels: 35.7 us -> 33.5 us  [local(): pl.pallas_call(functools.partial(kernel, n_dp, n_tile, ch, nx, hy), out_s...]
where the time goes in v3:
time: 35.8 us; the launch traced here: 35.6 us
  Pallas kernels  34.9 us (97%)
  between operations  0.66 us (2%)
    pallas_call x1, Pallas kernels, local(): pl.pallas_call(functools.partial(kernel, n_dp, n_tile, ch, nx, hy), out_s...  33.5 us
    pallas_call x1, Pallas kernels, local(): pl.pallas_call(functools.partial(unpack, ch, rows_half), out_shape=(jax.S...  1.42 us

profile of v3, /device:TPU:0, one launch (start us, length us, event | category | flops | bytes accessed | tf_op | source)
XLA Modules:
  0.0 35.6 jit_solution(15084697424311522438)
XLA Ops:
  0.6 33.5 %shard_map.118 = (bf16[64,1024]{1,0:T(8,128)(2,1)S(1)}, bf16[64,1024]{1,0:T(8,128)(2,1)S(1)}, bf16[2,1024,128]{2,1,0:T(8,128)(2,1)S(1)}, f32[8,64]{1,0:T(8,128)S(1)}) custom-call(bf16[64,8,128]{2,1,0:T(8,128)(2,1)} %bitcast.23, bf16[64,8,128]{2,1,0:T(8,128)(2,1)} %bitcast.24, s32[1,2]{1,0:T(1,128)} %bitcast.25, bf16[1728,64]{1,0:T(8,128)(2,1)} %bitcast.21, ...), custom_call_target="tpu_custom_call" | custom-call | tf_op jit(solution)/shard_map/pallas_call | solution.py:478
  34.2 1.4 %shard_map.119 = (bf16[64,8,128]{2,1,0:T(8,128)(2,1)}, bf16[64,8,128]{2,1,0:T(8,128)(2,1)}, f32[1728,64]{1,0:T(8,128)}, f32[1728,64]{1,0:T(8,128)}, f32[1,64]{1,0:T(1,128)}, /*index=5*/f32[1,64]{1,0:T(1,128)}) custom-call(bf16[64,8,128]{2,1,0:T(8,128)(2,1)S(1)} %bitcast.17, bf16[64,8,128]{2,1,0:T(8,128)(2,1)S(1)} %bitcast.18, ...), custom_call_target="tpu_custom_call" | custom-call | tf_op jit(solution)/shard_map/pallas_call | solution.py:524
  (2 shorter events, 0.0 us)

commit v4 on v3

--- a/solution.py
+++ b/solution.py
@@ -43,12 +43,15 @@
         lax.fori_loop(1, count, step, 0, unroll=count <= 32)
 
     def peer(k):
-        other = lax.rem(me + k, n_all)
+        other = lax.rem(me + jnp.where(2 * me < n_all, n_all - k, k), n_all)
         return (other // n_tile, lax.rem(other, n_tile))
 
-    def chip_peer(k):
-        other = lax.rem(chip + k, n_chips)
-        return other, (other // n_z, lax.rem(other, n_z) * 2 + core)
+    def on_chip(c):
+        return (c // n_z, lax.rem(c, n_z) * 2 + core)
+
+    far_first = [
+        d * n_z + k for d in reversed(range(n_dp))
+        for k in sorted(range(n_z), key=lambda k: (k == 0, abs(k - n_z // 2))) if d or k]
 
     sibling = (dp, z * 2 + 1 - core)
     has_left, has_right = tile > 0, tile < n_tile - 1
@@ -265,14 +268,13 @@
         half[g, pl.ds(0, rows_core[g]), :] = add_core(g).astype(BF16)
         here = jnp.where(core == 0, owners[g][0], owners[g][1])
 
-        def step(k):
-            other, device = chip_peer(k)
+        for k in far_first:
+            other = lax.rem(dp + k // n_z, n_dp) * n_z + lax.rem(z + k, n_z)
 
             @pl.when(other < here)
             def _():
-                send(g, 1, half.at[g, span(other * size, size, size), :], r1.at[g, k - 1], device)
-
-        each(n_chips, step)
+                send(g, 1, half.at[g, span(other * size, size, size), :], r1.at[g, k - 1],
+                     on_chip(other))
 
     def sum_chips(g, owned):
         place = q4.at[g, span(core * rows_core[g] + chip * size, size, size), :]
@@ -294,7 +296,8 @@
         def body(owned, count):
             if owned:
                 place = sum_chips(g, owned)
-                each(n_chips, lambda k: send(g, 2, place, place, chip_peer(k)[1]))
+                each(n_chips, lambda k: send(
+                    g, 2, place, place, on_chip(k - jnp.where(k > chip, 0, 1))))
         by_core(g, body)
 
     def gather_core(g):

time: 35.8 us -> 35.2 us (0.983)
  Pallas kernels: 34.9 us -> 34.4 us
    pallas_call x1, Pallas kernels: 33.5 us -> 33 us  [local(): pl.pallas_call(functools.partial(kernel, n_dp, n_tile, ch, nx, hy), out_s...]
where the time goes in v4:
time: 35.2 us; the launch traced here: 35.1 us
  Pallas kernels  34.4 us (98%)
  between operations  0.66 us (2%)
    pallas_call x1, Pallas kernels, local(): pl.pallas_call(functools.partial(kernel, n_dp, n_tile, ch, nx, hy), out_s...  33 us
    pallas_call x1, Pallas kernels, local(): pl.pallas_call(functools.partial(unpack, ch, rows_half), out_shape=(jax.S...  1.42 us

profile of v4, /device:TPU:0, one launch (start us, length us, event | category | flops | bytes accessed | tf_op | source)
XLA Modules:
  0.0 35.1 jit_solution(16957668089382516669)
XLA Ops:
  0.6 33.0 %shard_map.118 = (bf16[64,1024]{1,0:T(8,128)(2,1)S(1)}, bf16[64,1024]{1,0:T(8,128)(2,1)S(1)}, bf16[2,1024,128]{2,1,0:T(8,128)(2,1)S(1)}, f32[8,64]{1,0:T(8,128)S(1)}) custom-call(bf16[64,8,128]{2,1,0:T(8,128)(2,1)} %bitcast.23, bf16[64,8,128]{2,1,0:T(8,128)(2,1)} %bitcast.24, s32[1,2]{1,0:T(1,128)} %bitcast.25, bf16[1728,64]{1,0:T(8,128)(2,1)} %bitcast.21, ...), custom_call_target="tpu_custom_call" | custom-call | tf_op jit(solution)/shard_map/pallas_call | solution.py:481
  33.6 1.4 %shard_map.119 = (bf16[64,8,128]{2,1,0:T(8,128)(2,1)}, bf16[64,8,128]{2,1,0:T(8,128)(2,1)}, f32[1728,64]{1,0:T(8,128)}, f32[1728,64]{1,0:T(8,128)}, f32[1,64]{1,0:T(1,128)}, /*index=5*/f32[1,64]{1,0:T(1,128)}) custom-call(bf16[64,8,128]{2,1,0:T(8,128)(2,1)S(1)} %bitcast.17, bf16[64,8,128]{2,1,0:T(8,128)(2,1)S(1)} %bitcast.18, ...), custom_call_target="tpu_custom_call" | custom-call | tf_op jit(solution)/shard_map/pallas_call | solution.py:527
  (2 shorter events, 0.0 us)

commit v5 on v4

--- a/solution.py
+++ b/solution.py
@@ -21,6 +21,7 @@
     so_ref, ig_ref, q4, sums_out,
     occ_ref, k1_ref, k2_ref, gain_ref, shift_ref, raw, tall, in_sem,
     w1_ref, w2_ref, w1f_ref, w2f_ref, xd_pad, a_pad, i_pad, s_x, s_d, s_t, d3, ar, part, rp, half, r1,
+    xs_pad, s_xs, d3s, zn, zns, pair_s, pair_r,
     halo_s, halo_r, ar_s, ar_r, rs_s, rs_r,
 ):
     n_z = n_tile // 2
@@ -174,14 +175,14 @@
 
     nt = (((1,), (1,)), ((), ()))
 
-    def grad_by_input(stack, g, which):
+    def grad_by_input(g):
         count = 9 * ch // 2
         side = count // 2
-        first = which * rows_core[g]
-        found = lax.dot_general(
-            stack[span(which * count, count, 16), :], d3[...], nt, preferred_element_type=F32)
-        part[g, span(first, count, 8), :] = found[:, :2 * ch]
-        part[g, span(first + count, side, 8), :] = jnp.concatenate(
+        rows = span(core * count, count, 16)
+        found = (lax.dot_general(s_x[rows, :], d3[...], nt, preferred_element_type=F32)
+                 + lax.dot_general(s_xs[rows, :], d3s[...], nt, preferred_element_type=F32))
+        rp[g, pl.ds(0, count), :] = found[:, :2 * ch]
+        rp[g, pl.ds(count, side), :] = jnp.concatenate(
             [found[:side, 2 * ch:], found[side:, 2 * ch:]], axis=1)
 
     def grad_by_output(stack, g):
@@ -189,16 +190,16 @@
         side = rows // 2
         found = lax.dot_general(d3[...], stack[...], nt, preferred_element_type=F32)
         for m in range(4):
-            part[g, pl.ds(m * rows, rows), :] = found[:, m * 2 * ch:(m + 1) * 2 * ch]
-        part[g, pl.ds(4 * rows, side), :] = jnp.concatenate(
+            part[pl.ds(m * rows, rows), :] = found[:, m * 2 * ch:(m + 1) * 2 * ch]
+        part[pl.ds(4 * rows, side), :] = jnp.concatenate(
             [found[:side, 8 * ch:], found[side:, 8 * ch:]], axis=1)
 
     def span(start, count, step):
         return pl.ds(pl.multiple_of(start, step), count)
 
-    def put_d3(value):
+    def put_d3(value, out):
         for a in range(3):
-            d3[pl.ds(a * ch, ch), pl.ds(a * hy, flat)] = value
+            out[pl.ds(a * ch, ch), pl.ds(a * hy, flat)] = value
 
     def to_rows(columns):
         spot = lax.broadcasted_iota(jnp.int32, (ch, LANES), 1)
@@ -252,20 +253,24 @@
 
     def scatter_core(g):
         rows = rows_core[g]
-        send(g, 0, part.at[g, span((1 - core) * rows, rows, size), :], rp.at[g, pl.ds(0, rows), :],
+        send(g, 0, part.at[span((1 - core) * rows, rows, size), :], rp.at[g, pl.ds(0, rows), :],
              sibling)
+
+    def pair(index, src, dst):
+        return pltpu.make_async_remote_copy(
+            src_ref=src, dst_ref=dst, send_sem=pair_s.at[index], recv_sem=pair_r.at[index],
+            device_id=sibling, device_id_type=MESH)
 
     def add_core(g):
         rows = rows_core[g]
         done = rp.at[g, pl.ds(0, rows), :]
         settle(g, 0, done)
         drain(g, 0, done)
-        total = part[g, span(core * rows, rows, size), :] + rp[g, pl.ds(0, rows), :]
+        total = part[span(core * rows, rows, size), :] + rp[g, pl.ds(0, rows), :]
         rp[g, pl.ds(0, rows), :] = total
-        return total
 
     def scatter_chips(g):
-        half[g, pl.ds(0, rows_core[g]), :] = add_core(g).astype(BF16)
+        half[g, pl.ds(0, rows_core[g]), :] = rp[g, pl.ds(0, rows_core[g]), :].astype(BF16)
         here = jnp.where(core == 0, owners[g][0], owners[g][1])
 
         for k in far_first:
@@ -368,19 +373,25 @@
     rows = to_rows([sums_here, squares_here])
     small_start(0, rows[0:1], rows[1:2], jnp.broadcast_to(count_here, (1, ch)))
 
+    pair_x = pair(0, xd_pad.at[pl.ds(0, ch), :], xs_pad)
+    pair_x.start()
     shifts(xd_pad, ch, s_d)
     as_flipped(k2_ref, w2f_ref)
     act_grad = conv(w2f_ref, s_d)
     gain_shift = to_columns(jnp.concatenate(
         [gain_ref[...], shift_ref[...], jnp.zeros((6, ch), F32)], axis=0))
     d3[...] = jnp.zeros(d3.shape, d3.dtype)
-    for g, (first, last) in ((0, (used, 2 * rows_core[0])),
-                             (1, (used // 2, rows_core[1])),
-                             (1, (rows_core[1] + used // 2, 2 * rows_core[1]))):
-        if last > first:
-            part[g, pl.ds(first, last - first), :] = jnp.zeros((last - first, LANES), F32)
+    d3s[...] = jnp.zeros(d3s.shape, d3s.dtype)
+    if part.shape[0] > used:
+        part[pl.ds(used, part.shape[0] - used), :] = jnp.zeros((part.shape[0] - used, LANES), F32)
+    if rows_core[1] > used // 2:
+        rp[1, pl.ds(used // 2, rows_core[1] - used // 2), :] = jnp.zeros(
+            (rows_core[1] - used // 2, LANES), F32)
     as_matrix(k2_ref, w2_ref)
     as_flipped(k1_ref, w1f_ref)
+
+    pair_x.wait()
+    shifts(xs_pad, 0, s_xs)
 
     moments = to_columns(merge_moments(*small_end(0)))
     count = moments[:, 2:3]
@@ -396,13 +407,19 @@
     rows = to_rows([shift_here, gain_here])
     small_start(1, rows[0:1], rows[1:2], rows[0:1])
 
+    zn[pl.ds(0, ch), :] = z_grad
+    zn[pl.ds(ch, ch), :] = normal
+    zn[pl.ds(2 * ch, 8), :] = jnp.broadcast_to(mask, (8, flat))
+    pair_z = pair(1, zn, zns)
+    pair_z.start()
     act = (pre_act * sg * mask).astype(BF16)
     a_pad[:, pl.ds(hy, flat)] = act
     end_act = halo(1, a_pad, hy, a_pad)
-    put_d3(act)
+    put_d3(act, d3)
     grad_by_output(s_d, 0)
     scatter_core(0)
     shifts(a_pad, 0, s_t, outer=False)
+    add_core(0)
     scatter_chips(0)
     end_act()
     shifts(a_pad, 0, s_t, inner=False)
@@ -413,23 +430,26 @@
     totals = jnp.concatenate([totals[:, :ch], totals[:, ch:], jnp.zeros((6, ch), F32)], axis=0)
     sums_out[...] = totals
     totals = to_columns(totals)
-    delta_one = (gain * inv_std * (
-        z_grad - totals[:, 0:1] / count - normal * (totals[:, 1:2] / count)) * mask).astype(BF16)
+    def delta(z_grad, normal, mask):
+        return (gain * inv_std * (
+            z_grad - totals[:, 0:1] / count - normal * (totals[:, 1:2] / count)) * mask).astype(BF16)
+
+    delta_one = delta(z_grad, normal, mask)
     i_pad[:, pl.ds(hy, flat)] = delta_one
     end_delta = halo(2, i_pad, hy, i_pad)
-    put_d3(delta_one)
-    grad_by_input(s_x, 1, 1 - core)
-    scatter_core(1)
-    grad_by_input(s_x, 1, core)
+    put_d3(delta_one, d3)
+    pair_z.wait()
+    put_d3(delta(zns[pl.ds(0, ch), :], zns[pl.ds(ch, ch), :], zns[pl.ds(2 * ch, 1), :]), d3s)
+    grad_by_input(1)
+    scatter_chips(1)
     gather_line(0)
-    scatter_chips(1)
     shifts(i_pad, 0, s_t, outer=False)
     end_delta()
     shifts(i_pad, 0, s_t, inner=False)
     back = conv(w1f_ref, s_t)
     ig_ref[...] = ((xd_pad[pl.ds(ch, ch), pl.ds(hy, flat)].astype(F32) + back) * mask).astype(BF16)
+    gather_chips(1)
     gather_plane(0)
-    gather_chips(1)
     end_plane(0)
     gather_core(0)
     end_chips(1)
@@ -509,10 +529,16 @@
             pltpu.VMEM((9 * ch, flat + 2 * hy), BF16),
             pltpu.VMEM((3 * ch, flat + 2 * hy), BF16),
             pltpu.VMEM((2, n_all, 2, LANES), F32),
-            pltpu.VMEM((2, rows, LANES), F32),
+            pltpu.VMEM((rows, LANES), F32),
             pltpu.VMEM((2, rows // 2, LANES), F32),
             pltpu.VMEM((2, rows // 2, LANES), BF16),
             pltpu.VMEM((2, n_chips - 1, size, LANES), BF16),
+            pltpu.VMEM((ch, flat + 2 * hy), BF16),
+            pltpu.VMEM((9 * ch, flat + 2 * hy), BF16),
+            pltpu.VMEM((3 * ch, flat + 2 * hy), BF16),
+            pltpu.VMEM((2 * ch + 8, flat), F32),
+            pltpu.VMEM((2 * ch + 8, flat), F32),
+            dma((2,)), dma((2,)),
             dma((3, 2)), dma((3, 2)),
             dma((2,)), dma((2,)),
             dma((2, 6)), dma((2, 6)),

time: 35.2 us -> 33.6 us (0.955)
  Pallas kernels: 34.4 us -> 32.8 us
    pallas_call x1, Pallas kernels: 33 us -> 31.3 us  [local(): pl.pallas_call(functools.partial(kernel, n_dp, n_tile, ch, nx, hy), out_s...]
where the time goes in v5:
time: 33.6 us; the launch traced here: 33.4 us
  Pallas kernels  32.8 us (98%)
  between operations  0.66 us (2%)
    pallas_call x1, Pallas kernels, local(): pl.pallas_call(functools.partial(kernel, n_dp, n_tile, ch, nx, hy), out_s...  31.3 us
    pallas_call x1, Pallas kernels, local(): pl.pallas_call(functools.partial(unpack, ch, rows_half), out_shape=(jax.S...  1.42 us

profile of v5, /device:TPU:0, one launch (start us, length us, event | category | flops | bytes accessed | tf_op | source)
XLA Modules:
  0.0 33.4 jit_solution(2529651890922722442)
XLA Ops:
  0.6 31.3 %shard_map.118 = (bf16[64,1024]{1,0:T(8,128)(2,1)S(1)}, bf16[64,1024]{1,0:T(8,128)(2,1)S(1)}, bf16[2,1024,128]{2,1,0:T(8,128)(2,1)S(1)}, f32[8,64]{1,0:T(8,128)S(1)}) custom-call(bf16[64,8,128]{2,1,0:T(8,128)(2,1)} %bitcast.23, bf16[64,8,128]{2,1,0:T(8,128)(2,1)} %bitcast.24, s32[1,2]{1,0:T(1,128)} %bitcast.25, bf16[1728,64]{1,0:T(8,128)(2,1)} %bitcast.21, ...), custom_call_target="tpu_custom_call" | custom-call | tf_op jit(solution)/shard_map/pallas_call | solution.py:501
  32.0 1.4 %shard_map.119 = (bf16[64,8,128]{2,1,0:T(8,128)(2,1)}, bf16[64,8,128]{2,1,0:T(8,128)(2,1)}, f32[1728,64]{1,0:T(8,128)}, f32[1728,64]{1,0:T(8,128)}, f32[1,64]{1,0:T(1,128)}, /*index=5*/f32[1,64]{1,0:T(1,128)}) custom-call(bf16[64,8,128]{2,1,0:T(8,128)(2,1)S(1)} %bitcast.17, bf16[64,8,128]{2,1,0:T(8,128)(2,1)S(1)} %bitcast.18, ...), custom_call_target="tpu_custom_call" | custom-call | tf_op jit(solution)/shard_map/pallas_call | solution.py:553
  (2 shorter events, 0.0 us)

commit v6 on v5

--- a/solution.py
+++ b/solution.py
@@ -211,9 +211,8 @@
     def to_columns(rows):
         return jnp.transpose(jnp.concatenate([rows, jnp.zeros((LANES - 8, ch), F32)], axis=0))
 
-    def small_start(call, first, second, third):
-        ar[call, me, 0:1, :] = jnp.concatenate([first, second], axis=1)
-        ar[call, me, 1:2, :] = jnp.concatenate([third, third], axis=1)
+    def small_start(call, first, second):
+        ar[call, me] = jnp.concatenate([first, second], axis=1)
         each(n_all, lambda k: pltpu.make_async_remote_copy(
             src_ref=ar.at[call, me], dst_ref=ar.at[call, me],
             send_sem=ar_s.at[call], recv_sem=ar_r.at[call],
@@ -223,7 +222,7 @@
         arrived = ar.at[call, pl.ds(0, n_all - 1)]
         pltpu.make_async_copy(arrived, arrived, ar_r.at[call]).wait()
         pltpu.make_async_copy(arrived, arrived, ar_s.at[call]).wait()
-        return ar[call, :, 0, :], ar[call, :, 1, :]
+        return ar[call, :, 0, :]
 
     def merge_moments(sums_squares, counts):
         total = jnp.sum(sums_squares, axis=0, keepdims=True)
@@ -352,6 +351,9 @@
         drain(g, 5, others)
 
     end_xd = halo(0, xd_pad, hy, xd_pad)
+    count_here = jnp.sum(mask, axis=1, keepdims=True)
+    counts = jnp.broadcast_to(count_here, (1, ch))
+    small_start(2, counts, counts)
     shifts(xd_pad, 0, s_x, outer=False)
     zero_ends(xd_pad)
     zero_ends(a_pad)
@@ -366,12 +368,11 @@
     pre = (inside[ch:2 * ch]
            + jnp.concatenate([before, inside[:ch, :flat - hy]], axis=1)
            + jnp.concatenate([inside[2 * ch:, hy:], after], axis=1))
-    count_here = jnp.sum(mask, axis=1, keepdims=True)
     sums_here = jnp.sum(pre * mask, axis=1, keepdims=True)
     off = (pre - sums_here / jnp.maximum(count_here, 1.0)) * mask
     squares_here = jnp.sum(off * off, axis=1, keepdims=True)
     rows = to_rows([sums_here, squares_here])
-    small_start(0, rows[0:1], rows[1:2], jnp.broadcast_to(count_here, (1, ch)))
+    small_start(0, rows[0:1], rows[1:2])
 
     pair_x = pair(0, xd_pad.at[pl.ds(0, ch), :], xs_pad)
     pair_x.start()
@@ -393,7 +394,7 @@
     pair_x.wait()
     shifts(xs_pad, 0, s_xs)
 
-    moments = to_columns(merge_moments(*small_end(0)))
+    moments = to_columns(merge_moments(small_end(0), small_end(2)))
     count = moments[:, 2:3]
     mean = moments[:, 0:1] / count
     inv_std = lax.rsqrt(moments[:, 1:2] / count + EPSILON)
@@ -405,7 +406,7 @@
     shift_here = jnp.sum(z_grad, axis=1, keepdims=True)
     gain_here = jnp.sum(z_grad * normal, axis=1, keepdims=True)
     rows = to_rows([shift_here, gain_here])
-    small_start(1, rows[0:1], rows[1:2], rows[0:1])
+    small_start(1, rows[0:1], rows[1:2])
 
     zn[pl.ds(0, ch), :] = z_grad
     zn[pl.ds(ch, ch), :] = normal
@@ -426,7 +427,7 @@
     pre_two = conv(w2_ref, s_t)
     so_ref[...] = ((xd_pad[pl.ds(0, ch), pl.ds(hy, flat)].astype(F32) + pre_two) * mask).astype(BF16)
 
-    totals = jnp.sum(small_end(1)[0], axis=0, keepdims=True)
+    totals = jnp.sum(small_end(1), axis=0, keepdims=True)
     totals = jnp.concatenate([totals[:, :ch], totals[:, ch:], jnp.zeros((6, ch), F32)], axis=0)
     sums_out[...] = totals
     totals = to_columns(totals)
@@ -528,7 +529,7 @@
             pltpu.VMEM((9 * ch, flat + 2 * hy), BF16),
             pltpu.VMEM((9 * ch, flat + 2 * hy), BF16),
             pltpu.VMEM((3 * ch, flat + 2 * hy), BF16),
-            pltpu.VMEM((2, n_all, 2, LANES), F32),
+            pltpu.VMEM((3, n_all, 1, LANES), F32),
             pltpu.VMEM((rows, LANES), F32),
             pltpu.VMEM((2, rows // 2, LANES), F32),
             pltpu.VMEM((2, rows // 2, LANES), BF16),
@@ -540,7 +541,7 @@
             pltpu.VMEM((2 * ch + 8, flat), F32),
             dma((2,)), dma((2,)),
             dma((3, 2)), dma((3, 2)),
-            dma((2,)), dma((2,)),
+            dma((3,)), dma((3,)),
             dma((2, 6)), dma((2, 6)),
         ],
         compiler_params=pltpu.CompilerParams(

time: 33.6 us -> 33.3 us (level)
  no operation moved by 1% of the time
where the time goes in v6:
time: 33.3 us; the launch traced here: 33.2 us
  Pallas kernels  32.5 us (98%)
  between operations  0.66 us (2%)
    pallas_call x1, Pallas kernels, local(): pl.pallas_call(functools.partial(kernel, n_dp, n_tile, ch, nx, hy), out_s...  31.1 us
    pallas_call x1, Pallas kernels, local(): pl.pallas_call(functools.partial(unpack, ch, rows_half), out_shape=(jax.S...  1.42 us

profile of v6, /device:TPU:0, one launch (start us, length us, event | category | flops | bytes accessed | tf_op | source)
XLA Modules:
  0.0 33.2 jit_solution(7923248153862724820)
XLA Ops:
  0.6 31.1 %shard_map.118 = (bf16[64,1024]{1,0:T(8,128)(2,1)S(1)}, bf16[64,1024]{1,0:T(8,128)(2,1)S(1)}, bf16[2,1024,128]{2,1,0:T(8,128)(2,1)S(1)}, f32[8,64]{1,0:T(8,128)S(1)}) custom-call(bf16[64,8,128]{2,1,0:T(8,128)(2,1)} %bitcast.23, bf16[64,8,128]{2,1,0:T(8,128)(2,1)} %bitcast.24, s32[1,2]{1,0:T(1,128)} %bitcast.25, bf16[1728,64]{1,0:T(8,128)(2,1)} %bitcast.21, ...), custom_call_target="tpu_custom_call" | custom-call | tf_op jit(solution)/shard_map/pallas_call | solution.py:502
  31.8 1.4 %shard_map.119 = (bf16[64,8,128]{2,1,0:T(8,128)(2,1)}, bf16[64,8,128]{2,1,0:T(8,128)(2,1)}, f32[1728,64]{1,0:T(8,128)}, f32[1728,64]{1,0:T(8,128)}, f32[1,64]{1,0:T(1,128)}, /*index=5*/f32[1,64]{1,0:T(1,128)}) custom-call(bf16[64,8,128]{2,1,0:T(8,128)(2,1)S(1)} %bitcast.17, bf16[64,8,128]{2,1,0:T(8,128)(2,1)S(1)} %bitcast.18, ...), custom_call_target="tpu_custom_call" | custom-call | tf_op jit(solution)/shard_map/pallas_call | solution.py:554
  (2 shorter events, 0.0 us)
